TPU v7x, 32 devices: a whole 2x2x4 slice. The times are simulated.
32 devices in a mesh: ctx: 16 (over z, y, x), ch: 2 (over core).
Axes of the slice: x: 2, y: 2, z: 4, core: 2. Of those that a mesh axis runs over, the one named last changes fastest.
Arguments:
- grad_out: bfloat16 [12288, 4096], P('ctx', 'ch'), may hold values from -6 to 6
- block_input: bfloat16 [12288, 4096], P('ctx', 'ch'), may hold values from -40 to 40
- norm_gain: bfloat16 [4096], P('ch'), may hold values from 0.5 to 1.5
- queries: bfloat16 [12288, 4096], P('ctx', 'ch'), may hold values from -6 to 6
- keys: bfloat16 [12288, 4096], P('ctx', 'ch'), may hold values from -6 to 6
- values: bfloat16 [12288, 4096], P('ctx', 'ch'), may hold values from -6 to 6
- filters: bfloat16 [256, 128], P('ch'), may hold values from -0.5 to 0.5
- doc_starts: int32 [16, 4], P('ctx'), may hold values from 0 to 767, as said below
- in_weight: bfloat16 [4096, 3, 4096], P('ctx', None, 'ch'), may hold values from -0.09375 to 0.09375
- out_weight: bfloat16 [4096, 4096], P('ch', 'ctx'), may hold values from -0.09375 to 0.09375
Outputs:
- grad_input: bfloat16 [12288, 4096], P('ctx', 'ch')
Inputs may be any that keep to these rules, and one draw needn't show every extreme that they name: `doc_starts`: each row holds 4 distinct document starts of one slab as offsets within the slab, in ascending order; the first slab's first start is 0.
All inputs are finite; a program needn't handle non-finite values.
Results may differ from a plain program's by a relative error of at most 0.013.
Values may be sent and summed in bfloat16 or wider, within the bound.
No kernel may reach another device: no remote copies, remote signals or barrier semaphores. Data moves between devices by JAX's collectives and lax.ppermute only.
A program may use at most 192 MiB of HBM per device.

v0:
```python
import functools

import jax
import jax.numpy as jnp
from jax import lax
from jax.experimental import pallas as pl
from jax.experimental.pallas import tpu as pltpu
from jax.sharding import Mesh
from jax.sharding import PartitionSpec as P

LANES = 128
EPSILON = 1e-05
VMEM_BYTES = 48 * 1024 * 1024

BRIEF = pl.CostEstimate(flops=1024, bytes_accessed=1024, transcendentals=0)

SWAP = [(1, 2), (2, 1)]
CYCLE = [(0, 2), (1, 0), (2, 3), (3, 1)]
PAIR = [(0, 1), (1, 0)]


def fence(*blocks):
    return lax.optimization_barrier(blocks)


def params(parallel):
    return pltpu.CompilerParams(
        dimension_semantics=("arbitrary",) * parallel, vmem_limit_bytes=VMEM_BYTES
    )


def toeplitz_into(table_ref, base_ref, taps, count):
    for q in range(count):
        row = jnp.broadcast_to(base_ref[q : q + 1, :], (taps, 2 * taps))
        band = pltpu.roll(row, 0, 1, stride=1, stride_axis=0)
        table_ref[q * taps : (q + 1) * taps, :] = band.astype(table_ref.dtype)


def banded(table, keep, source, taps, count):
    table = table.reshape(count, taps, 2 * taps)
    masked = (table * keep[None]).reshape(count * taps, 2 * taps)
    wide = jnp.dot(masked, source, preferred_element_type=jnp.float32)
    width = source.shape[1]
    owner = lax.broadcasted_iota(jnp.int32, (taps, width), 1) // (width // count)
    total = wide[:taps]
    for q in range(1, count):
        total = jnp.where(owner == q, wide[q * taps : (q + 1) * taps], total)
    return total


def forward_kernel(
    taps, count, base_ref, last_ref, tail_ref, keys_ref, values_ref, mix_ref, conv_ref,
    q_ref, k_ref, table_ref, source_ref,
):
    rows, width = keys_ref.shape
    parts = width // LANES
    toeplitz_into(table_ref, base_ref, taps, parts * count)
    values = values_ref[...].astype(jnp.float32)
    source_ref[:taps, :] = tail_ref[...]
    source_ref[taps:, :] = (keys_ref[...].astype(jnp.float32) * values).astype(jnp.bfloat16)
    k_ref[...] = (conv_ref[...] * values).astype(k_ref.dtype)

    def tile(i, carry):
        row = pl.multiple_of(i * taps, taps)
        col = lax.broadcasted_iota(jnp.int32, (taps, 2 * taps), 1) + (i - 1) * taps
        keep = jnp.where(col >= last_ref[pl.ds(row, taps), :], 1.0, 0.0).astype(jnp.bfloat16)
        for p in range(parts):
            lanes = slice(p * LANES, (p + 1) * LANES)
            table = table_ref[p * count * taps : (p + 1) * count * taps, :]
            mixed = banded(table, keep, source_ref[pl.ds(row, 2 * taps), lanes], taps, count)
            at = (pl.ds(row, taps), lanes)
            q_ref[at] = (mix_ref[at] * mixed).astype(q_ref.dtype)
        return carry

    lax.fori_loop(0, rows // taps, tile, 0)


def backward_kernel(
    taps, count, base_ref, last_ref, head_ref, keys_ref, queries_ref, mix_ref,
    conv_ref, v_ref, table_ref, source_ref,
):
    rows, width = keys_ref.shape
    parts = width // LANES
    toeplitz_into(table_ref, base_ref, taps, parts * count)
    source_ref[:rows, :] = (mix_ref[...] * queries_ref[...].astype(jnp.float32)).astype(jnp.bfloat16)
    source_ref[rows:, :] = head_ref[...]

    def tile(i, carry):
        row = pl.multiple_of(i * taps, taps)
        at_row = lax.broadcasted_iota(jnp.int32, (taps, 2 * taps), 0) + i * taps
        keep = jnp.where(at_row >= last_ref[:, pl.ds(row, 2 * taps)], 1.0, 0.0).astype(jnp.bfloat16)
        for p in range(parts):
            lanes = slice(p * LANES, (p + 1) * LANES)
            table = table_ref[p * count * taps : (p + 1) * count * taps, :]
            conv = banded(table, keep, source_ref[pl.ds(row, 2 * taps), lanes], taps, count)
            at = (pl.ds(row, taps), lanes)
            conv_ref[at] = conv
            v_ref[at] = (conv * keys_ref[at].astype(jnp.float32)).astype(v_ref.dtype)
        return carry

    lax.fori_loop(0, rows // taps, tile, 0)


def conv_call(kernel, name, base, last, edge, operands, dtypes, taps, per):
    rows, width = operands[0].shape
    cols = min(width, 4 * LANES)
    count = cols // LANES * per
    slab = pl.BlockSpec((rows, cols), lambda g: (0, g))
    return pl.pallas_call(
        functools.partial(kernel, taps, per),
        grid=(width // cols,),
        in_specs=[
            pl.BlockSpec((count, 2 * taps), lambda g: (g, 0)),
            pl.BlockSpec(last.shape, lambda g: (0, 0)),
            pl.BlockSpec((taps, cols), lambda g: (0, g)),
        ]
        + [slab] * len(operands),
        out_specs=[slab] * len(dtypes),
        out_shape=[jax.ShapeDtypeStruct((rows, width), t) for t in dtypes],
        scratch_shapes=[
            pltpu.VMEM((count * taps, 2 * taps), jnp.bfloat16),
            pltpu.VMEM((rows + taps, cols), jnp.bfloat16),
        ],
        compiler_params=params(1),
        cost_estimate=BRIEF,
        name=name,
    )(base, last, edge, *operands)


NT = (((1,), (1,)), ((), ()))


def mix_kernel(at_ref, *refs):
    lefts, own_ref, sib_ref, out_ref = refs[:-3], *refs[-3:]
    step = pl.program_id(1)
    both = None
    for n, left in enumerate(lefts):
        right = (own_ref, sib_ref)[n % 2][n // 2]
        part = lax.dot_general(left[...], right, NT, preferred_element_type=jnp.float32)
        both = part if both is None else both + part

    @pl.when(step == 0)
    def _():
        out_ref[...] = both

    @pl.when(step > 0)
    def _():
        out_ref[...] += both


def mix_matmul(at, grads, own, sib):
    rows = grads.shape[0]
    blocks, width, feats = own.shape
    cols = min(width, 1024)
    lefts = [
        pl.BlockSpec((rows, feats), lambda n, j, at, side=side, k=k: (0, at[side, 2 * j + k]))
        for k in range(2)
        for side in range(2)
    ]
    right = pl.BlockSpec((2, cols, feats), lambda n, j, at: (j, n, 0))
    return pl.pallas_call(
        mix_kernel,
        grid_spec=pltpu.PrefetchScalarGridSpec(
            num_scalar_prefetch=1,
            grid=(width // cols, blocks // 2),
            in_specs=lefts + [right, right],
            out_specs=pl.BlockSpec((rows, cols), lambda n, j, at: (0, n)),
        ),
        out_shape=jax.ShapeDtypeStruct((rows, width), jnp.float32),
        compiler_params=params(2),
        cost_estimate=BRIEF,
        name="mix_matmul",
    )(at, *[grads] * len(lefts), own, sib)


def project_kernel(places, blocks, *refs):
    half = pl.num_programs(0) // 2
    own, sib = refs[: len(places)], refs[len(places) : 2 * len(places)]
    weights, outs = refs[2 * len(places) : -2], refs[-2:]

    def into(grads, out_ref):
        for n in range(blocks):
            total = None
            for grad, (b, left) in zip(grads, places):
                right = weights[n][b, :, left : left + grad.shape[1]]
                part = lax.dot_general(grad[...], right, NT, preferred_element_type=jnp.float32)
                total = part if total is None else total + part
            out_ref[n] = total.astype(out_ref.dtype)

    @pl.when(pl.program_id(0) < half)
    def _():
        into(own, outs[0])

    @pl.when(pl.program_id(0) >= half)
    def _():
        into(sib, outs[1])


def project(own, sib, weights):
    blocks = len(weights)
    branches, feats, width = weights[0].shape
    rows = own[0][0].shape[0]
    places = [
        (b, sum(p.shape[1] for p in pieces[:at])) for b, pieces in enumerate(own) for at in range(len(pieces))
    ]
    own, sib = [p for pieces in own for p in pieces], [p for pieces in sib for p in pieces]
    half = 2
    step = rows // half

    def first(i):
        return jnp.minimum(i, half - 1)

    def second(i):
        return jnp.maximum(i - half, 0)

    out = jax.ShapeDtypeStruct((blocks, rows, feats), jnp.bfloat16)
    return pl.pallas_call(
        functools.partial(project_kernel, places, blocks),
        grid=(2 * half,),
        in_specs=[pl.BlockSpec((step, p.shape[1]), lambda i: (first(i), 0)) for p in own]
        + [pl.BlockSpec((step, p.shape[1]), lambda i: (second(i), 0)) for p in sib]
        + [pl.BlockSpec((branches, feats, width), lambda i: (0, 0, 0))] * blocks,
        out_specs=[
            pl.BlockSpec((blocks, step, feats), lambda i: (0, first(i), 0)),
            pl.BlockSpec((blocks, step, feats), lambda i: (0, second(i), 0)),
        ],
        out_shape=[out, out],
        compiler_params=params(1),
        cost_estimate=BRIEF,
        name="project",
    )(*own, *sib, *weights)


def pick_kernel(at_ref, own_ref, sib_ref, input_ref, gain_ref, norm_ref, cross_ref):
    step = pl.program_id(0)
    ours = (lax.broadcasted_iota(jnp.int32, own_ref.shape[1:], 0) * 0 + at_ref[2, step]) == 1
    norm = jnp.where(ours, own_ref[0].astype(jnp.float32), sib_ref[0].astype(jnp.float32))
    norm_ref[...] = norm.astype(norm_ref.dtype)
    part = jnp.sum(
        gain_ref[...].astype(jnp.float32) * norm * input_ref[...].astype(jnp.float32),
        axis=1,
        keepdims=True,
    )

    @pl.when(step == 0)
    def _():
        cross_ref[...] = part

    @pl.when(step > 0)
    def _():
        cross_ref[...] += part


def pick(at, own, sib, block_input, gain):
    rows, width = block_input.shape
    feats = own.shape[2]
    return pl.pallas_call(
        pick_kernel,
        grid_spec=pltpu.PrefetchScalarGridSpec(
            num_scalar_prefetch=1,
            grid=(width // feats,),
            in_specs=[
                pl.BlockSpec((1, rows, feats), lambda j, at: (at[0, j], 0, 0)),
                pl.BlockSpec((1, rows, feats), lambda j, at: (at[1, j], 0, 0)),
                pl.BlockSpec((rows, feats), lambda j, at: (0, j)),
                pl.BlockSpec((1, feats), lambda j, at: (0, j)),
            ],
            out_specs=[
                pl.BlockSpec((rows, feats), lambda j, at: (0, j)),
                pl.BlockSpec((rows, 1), lambda j, at: (0, 0)),
            ],
        ),
        out_shape=[
            jax.ShapeDtypeStruct((rows, width), jnp.bfloat16),
            jax.ShapeDtypeStruct((rows, 1), jnp.float32),
        ],
        compiler_params=params(1),
        cost_estimate=BRIEF,
        name="pick",
    )(at, own, sib, block_input, gain)


def on_device(
    ring,
    n_chan,
    grad_out,
    block_input,
    norm_gain,
    queries,
    keys,
    values,
    filters,
    doc_starts,
    in_weight,
    out_weight,
):
    rows, width = grad_out.shape
    groups, taps = filters.shape
    feats, branches = in_weight.shape[:2]
    count = len(ring)
    per = LANES * groups // width
    features = feats * 2 * count
    o, x, h, c = (lax.axis_index(a) for a in ("o", "x", "h", "c"))
    order = jnp.array(ring, jnp.int32)
    place = jnp.array([ring.index(i) for i in range(count)], jnp.int32)
    position = place[o]
    far = count // 2
    forth = [(ring[i], ring[(i + 1) % count]) for i in range(count)]
    back = [(b, a) for a, b in forth]

    def exchanged(block):
        return lax.ppermute(block, ("x", "c"), SWAP)

    def swapped(block):
        return jnp.where(x == c, block, exchanged(block))

    def sibling(block):
        return lax.ppermute(block, "c", PAIR)

    def both_ways(up, down):
        return lax.ppermute(up, ("o",), forth), lax.ppermute(down, ("o",), back)

    def far_halves(up, down, axis):
        half = up.shape[axis] // 2
        return both_ways(
            lax.slice_in_dim(up, 0, half, axis=axis),
            lax.slice_in_dim(down, half, 2 * half, axis=axis),
        )

    all_starts = lax.all_gather(doc_starts, ("o", "x"), axis=0, tiled=True)
    taps32 = swapped(filters).astype(jnp.float32)
    out_w = swapped(out_weight)
    in_w = jnp.swapaxes(in_weight, 0, 1)
    out_w, in_w, grad_out, taps32 = fence(out_w, in_w, grad_out, taps32)

    in_recv = exchanged(in_w)
    blocks = [out_w]
    up = down = out_w
    for s in range(1, far):
        up, down = both_ways(up, down)
        if s == far - 2:
            up, down, in_recv, in_w, grad_out = fence(up, down, in_recv, in_w, grad_out)
        blocks += [up, down]
    in_w = jnp.where(x == c, in_w, in_recv)
    half_recv = exchanged(grad_out)
    blocks.append(jnp.concatenate(far_halves(up, down, 0), axis=0))
    own_out = jnp.stack(blocks)
    source_in = block_input.astype(jnp.float32)
    square_sum = jnp.sum(source_in * source_in, axis=1, keepdims=True)
    distances = [0] + [d for s in range(1, far) for d in (-s, s)] + [far]
    sources = order[(position + jnp.array(distances, jnp.int32)) % count]
    wide = width // feats

    def column(parity):
        block = sources * 2 + parity
        owner = block // wide
        side = jnp.where(owner % 2 == x, 0, 1)
        return side * (n_chan * wide) + (owner // 2) * wide + block % wide

    columns = jnp.stack([column(c), column(1 - c)])
    slabs = 2 * count
    slab = o * 2 + c
    onward = [(i, i + 1) for i in range(slabs - 1)]
    backward = [(i + 1, i) for i in range(slabs - 1)]
    positions = jnp.arange(rows, dtype=jnp.int32)

    def last_of(at):
        starts = all_starts[jnp.minimum(at, slabs - 1)]
        prior = jnp.where(at > 0, all_starts[jnp.maximum(at - 1, 0), -1], 0)
        own = jnp.where(starts[None, :] <= positions[:, None], starts[None, :], -rows)
        return jnp.maximum(jnp.max(own, axis=1), prior - rows)

    last_start = last_of(slab)
    padded_last = jnp.concatenate([last_start, last_of(slab + 1)[:taps] + rows])[None]
    edge = jnp.zeros((groups, taps), jnp.float32)
    base_back = jnp.concatenate([taps32, edge], axis=1)
    base_fore = jnp.concatenate([edge[:, :1], taps32[:, ::-1], edge[:, 1:]], axis=1)
    own_out, in_w, half_recv, grad_out, square_sum, padded_last, last_col, base_back, base_fore, columns = fence(
        own_out, in_w, half_recv, grad_out, square_sum, padded_last, last_start[:, None], base_back,
        base_fore, columns,
    )

    ahead, behind = {0: in_w}, {0: in_w}
    ahead[1], behind[1] = both_ways(in_w, in_w)
    sib_out = sibling(own_out)
    grad_other = lax.ppermute(grad_out, ("x", "c"), CYCLE)
    grad_other, keys = fence(grad_other, keys)
    k_recv = exchanged(keys)
    grad_half = jnp.where(x == c, grad_out, half_recv)
    if n_chan > 1:
        grad_half = lax.all_gather(grad_half, "h", axis=1, tiled=True)
        grad_other = lax.all_gather(grad_other, "h", axis=1, tiled=True)
    grads = jnp.concatenate([grad_half, grad_other], axis=1)
    mix_grad = mix_matmul(columns, grads, own_out, sib_out)
    ahead[1], behind[1], mix_grad, k_recv, queries = fence(
        ahead[1], behind[1], mix_grad, k_recv, queries
    )

    ahead[2], behind[2] = both_ways(ahead[1], behind[1])
    q_recv, queries, values, mix_grad = fence(exchanged(queries), queries, values, mix_grad)
    middle = width // 2
    parts = (slice(0, middle), slice(middle, width))
    v_recv = exchanged(values[:, parts[0]])
    own_k, own_q = jnp.where(x == c, keys, k_recv), jnp.where(x == c, queries, q_recv)
    head = (mix_grad[:taps] * own_q[:taps].astype(jnp.float32)).astype(jnp.bfloat16)
    head = lax.ppermute(head, ("o", "c"), backward)
    conv, v_grad = conv_call(
        backward_kernel, "backward_conv", base_back, padded_last, head,
        [own_k, own_q, mix_grad], [jnp.float32, jnp.bfloat16], taps, per,
    )
    v_recv, values, conv, v_grad = fence(v_recv, values, conv, v_grad)

    def forward(at, received):
        own_v = jnp.where(x == c, values[:, parts[at]], received)
        part_k = own_k[:, parts[at]]
        tail = part_k[rows - taps :].astype(jnp.float32) * own_v[rows - taps :].astype(jnp.float32)
        tail = lax.ppermute(tail.astype(jnp.bfloat16), ("o", "c"), onward)
        base = base_fore[at * groups // 2 : (at + 1) * groups // 2]
        return conv_call(
            forward_kernel, "forward_conv", base, last_col, tail,
            [part_k, own_v, mix_grad[:, parts[at]], conv[:, parts[at]]],
            [jnp.bfloat16, jnp.bfloat16], taps, per,
        )

    later = exchanged(values[:, parts[1]])
    q_left, k_left = forward(0, v_recv)
    sib_v = sibling(v_grad)
    ahead[2], behind[2], q_left, k_left, later, v_grad = fence(
        ahead[2], behind[2], q_left, k_left, later, v_grad
    )

    ahead[3], behind[3] = both_ways(ahead[2], behind[2])
    q_right, k_right = forward(1, later)
    own_grads = [[q_left, q_right], [k_left, k_right], [v_grad]]
    sib_grads = [[sibling(p) for p in pieces] for pieces in own_grads[:2]] + [[sib_v]]

    norms = []

    def add_blocks(weights):
        ours, theirs = project(own_grads, sib_grads, weights)
        keep = jnp.where(c == x, ours, theirs)
        send = jnp.where(c == x, theirs, ours)
        received = lax.ppermute(send, "x", PAIR)
        norms.append((keep.astype(jnp.float32) + received.astype(jnp.float32)).astype(jnp.bfloat16))

    for s in range(3, far + 1):
        if 3 < s < far:
            ahead[s], behind[s] = both_ways(ahead[s - 1], behind[s - 1])
        elif s == far:
            up, down = far_halves(ahead[s - 1], behind[s - 1], 1)
        if s == 3:
            add_blocks([in_w, ahead[1], behind[1]])
        add_blocks([ahead[s - 1], behind[s - 1]])
        if s < far:
            ahead[s], behind[s], norms[-1] = fence(ahead[s], behind[s], norms[-1])
        else:
            up, down, norms[-1] = fence(up, down, norms[-1])
    add_blocks([jnp.concatenate([up, down], axis=1)])
    if n_chan > 1:
        norm = jnp.concatenate(norms, axis=0)
        slot = jnp.zeros((count,), jnp.int32).at[sources].set(jnp.arange(count, dtype=jnp.int32))
        norm = lax.psum_scatter(
            jnp.take(norm, slot, axis=0), "h", scatter_dimension=0, tiled=True
        )
        other = lax.ppermute(norm, "c", PAIR)
        slot = jnp.arange(count, dtype=jnp.int32) - h * (count // n_chan)
    else:
        norm = jnp.concatenate(norms, axis=0)
        other = jnp.concatenate([lax.ppermute(n, "c", PAIR) for n in norms], axis=0)
        slot = jnp.zeros((count,), jnp.int32).at[sources].set(jnp.arange(count, dtype=jnp.int32))
    mine = (h * 2 + c) * wide + jnp.arange(wide, dtype=jnp.int32)
    slots = slot[mine // 2]
    at = jnp.stack([slots, slots, (mine % 2 == c).astype(jnp.int32)])
    norm_grad, cross = pick(at, norm, other, block_input, norm_gain[None])
    cross_sum, square_sum = lax.psum((cross, square_sum), ("h", "c"))
    inverse = lax.rsqrt(square_sum / features + EPSILON)
    scaled = norm_gain.astype(jnp.float32)[None, :] * norm_grad.astype(jnp.float32)
    result = (
        grad_out.astype(jnp.float32)
        + inverse * scaled
        - source_in * (inverse * inverse * inverse) * cross_sum / features
    )
    return result.astype(jnp.bfloat16)


def solution(mesh):
    outer, n_chan = mesh.shape["ctx"] // 2, mesh.shape["ch"] // 2
    split = Mesh(mesh.devices.reshape(outer, 2, n_chan, 2), ("o", "x", "h", "c"))
    ring = list(range(0, outer, 2)) + list(range(outer - 1, 0, -2))
    tok, chan = ("o", "x"), ("h", "c")
    placed = (
        P(tok, chan),
        P(tok, chan),
        P(chan),
        P(tok, chan),
        P(tok, chan),
        P(tok, chan),
        P(chan, None),
        P(tok, None),
        P(tok, None, chan),
        P(chan, tok),
    )
    return jax.shard_map(
        functools.partial(on_device, ring, n_chan),
        mesh=split,
        in_specs=placed,
        out_specs=P(tok, chan),
        check_vma=False,
    )
```

profile of v0, /device:TPU:0, one launch (start us, length us, event | category | flops | bytes accessed | tf_op | source)
XLA Modules:
  0.0 535.4 jit_solution(2971404877248150163)
XLA Ops:
  2.5 45.7 %all-gather = s32[16,1,4]{2,1,0:T(1,128)S(1)} all-gather(s32[1,1,4]{2,1,0:T(1,128)} %bitcast.66), channel_id=1, replica_groups=mesh['o'=8,'x'=2,'h'=1,'c'=2] {'o','x'}, dimensions={0}, use_global_device_ids=true | all-gather | bytes 272 | tf_op jit(solution)/shard_map/all_gather | solution.py:330
  61.3 19.0 %collective-permute-done.2 = bf16[2048,256]{1,0:T(8,128)(2,1)} collective-permute-done((bf16[2048,256]{1,0:T(8,128)(2,1)}, bf16[2048,256]{1,0:T(8,128)(2,1)}, u32[]{:S(2)}, u32[]{:S(2)}) %collective-permute-start.2) | collective-permute-done | bytes 1048608 | tf_op jit(solution)/shard_map/ppermute | solution.py:321
  87.0 16.8 %collective-permute-done.4 = bf16[2048,256]{1,0:T(8,128)(2,1)S(1)} collective-permute-done((bf16[2048,256]{1,0:T(8,128)(2,1)}, bf16[2048,256]{1,0:T(8,128)(2,1)S(1)}, u32[]{:S(2)}, u32[]{:S(2)}) %collective-permute-start.4) | collective-permute-done | bytes 1048608 | tf_op jit(solution)/shard_map/ppermute | solution.py:321
  111.8 21.1 %collective-permute-done.8 = bf16[2048,256]{1,0:T(8,128)(2,1)S(1)} collective-permute-done((bf16[2048,256]{1,0:T(8,128)(2,1)S(1)}, bf16[2048,256]{1,0:T(8,128)(2,1)S(1)}, u32[]{:S(2)}, u32[]{:S(2)}) %collective-permute-start.8) | collective-permute-done | bytes 1048608 | tf_op jit(solution)/shard_map/ppermute | solution.py:321
  137.1 9.2 %collective-permute-done.10 = bf16[1024,256]{1,0:T(8,128)(2,1)S(1)} collective-permute-done((bf16[1024,256]{1,0:T(8,128)(2,1)S(1)}, bf16[1024,256]{1,0:T(8,128)(2,1)S(1)}, u32[]{:S(2)}, u32[]{:S(2)}) %collective-permute-start.10) | collective-permute-done | bytes 524320 | tf_op jit(solution)/shard_map/ppermute | solution.py:321
  149.5 32.7 %collective-permute-done.14 = bf16[768,2048]{1,0:T(8,128)(2,1)S(1)} collective-permute-done((bf16[768,2048]{1,0:T(8,128)(2,1)S(1)}, bf16[768,2048]{1,0:T(8,128)(2,1)S(1)}, u32[]{:S(2)}, u32[]{:S(2)}) %collective-permute-start.14) | collective-permute-done | bytes 3145760 | tf_op jit(solution)/shard_map/ppermute | solution.py:386
  186.6 5.1 pad_maximum_fusion.refs_0_.refs_1_.refs_2_.refs_3_
  191.8 23.2 %mix_matmul.1.mix_ref = f32[768,2048]{1,0:T(8,128)} custom-call(s32[2,8]{1,0:T(2,128)S(1)} %pad_add_fusion.2.at_ref, bf16[768,4096]{1,0:T(8,128)(2,1)} %pad_maximum_fusion.refs_0_.refs_1_.refs_2_.refs_3_, bf16[768,4096]{1,0:T(8,128)(2,1)} %pad_maximum_fusion.refs_0_.refs_1_.refs_2_.refs_3_, ...), custom_call_target="tpu_custom_call" | custom-call | flops 1024 | bytes 1024 | tf_op jit(solution)/shard_map/mix_matmul/pallas_call | solution.py:161
  228.5 3.9 broadcast_select_fusion.1.keys_ref
  232.4 39.9 %collective-permute-done.21.head_ref = bf16[128,2048]{1,0:T(8,128)(2,1)S(1)} collective-permute-done((bf16[128,2048]{1,0:T(8,128)(2,1)S(1)}, bf16[128,2048]{1,0:T(8,128)(2,1)S(1)}, u32[]{:S(2)}, u32[]{:S(2)}) %collective-permute-start.21) | collective-permute-done | bytes 524320 | tf_op jit(solution)/shard_map/ppermute | solution.py:406
  272.2 24.2 %backward_conv.1 = (f32[768,2048]{1,0:T(8,128)}, bf16[768,2048]{1,0:T(8,128)(2,1)S(1)}) custom-call(f32[128,256]{1,0:T(8,128)S(1)} %concatenate.26.base_ref, s32[1,896]{1,0:T(1,128)S(1)} %broadcast_in_dim.41.last_ref, bf16[128,2048]{1,0:T(8,128)(2,1)S(1)} %collective-permute-done.21.head_ref, bf16[768,2048]{1,0:T(8,128)(2,1)} %broadcast_select_fusion.1.keys_ref, ...), custom_call_target="tpu_custom_call" | custom-call | flops 1024 | bytes 1024 | tf_op jit(solution)/shard_map/backward_conv/pallas_call | solution.py:109
  300.6 27.2 %collective-permute-start.29 = (bf16[768,2048]{1,0:T(8,128)(2,1)S(1)}, bf16[768,2048]{1,0:T(8,128)(2,1)}, u32[]{:S(2)}, u32[]{:S(2)}) collective-permute-start(bf16[768,2048]{1,0:T(8,128)(2,1)S(1)} %get-tuple-element.110.refs_4_), channel_id=1, source_target_pairs={{0,1},{1,0},{2,3},{3,2},{4,5},{5,4},{6,7},{7,6},{8,9},{9,8},{10,11... | collective-permute-start | bytes 9437192 | tf_op jit(solution)/shard_map/ppermute | solution.py:318
  331.0 6.7 %fusion.21 = (f32[768,1024]{1,0:T(8,128)}, f32[768,1024]{1,0:T(8,128)}) fusion(f32[768,2048]{1,0:T(8,128)} %mix_matmul.1.mix_ref), kind=kLoop, calls=%fused_computation.114 | loop fusion | bytes 12582912 | tf_op jit(solution)/shard_map/slice | solution.py:421
  344.2 15.1 %forward_conv.2 = (bf16[768,1024]{1,0:T(8,128)(2,1)S(1)}, bf16[768,1024]{1,0:T(8,128)(2,1)}) custom-call(f32[64,256]{1,0:T(8,128)S(1)} %copy-done.4, s32[768,1]{1,0:T(8,128)S(1)} %copy.18.last_ref, bf16[128,1024]{1,0:T(8,128)(2,1)S(1)} %collective-permute-done.22.tail_ref, bf16[768,1024]{1,0:T(8,128)(2,1)S(1)} %get-tuple-element.138.keys_ref, ...), custom_call_target="tpu_custom_call" | custom-call | flops 1024 | bytes 1024 | tf_op jit(solution)/shard_map/forward_conv/pallas_call | solution.py:109
  371.9 15.0 %forward_conv.3 = (bf16[768,1024]{1,0:T(8,128)(2,1)}, bf16[768,1024]{1,0:T(8,128)(2,1)}) custom-call(f32[64,256]{1,0:T(8,128)S(1)} %copy-done.3, s32[768,1]{1,0:T(8,128)S(1)} %copy.18.last_ref, bf16[128,1024]{1,0:T(8,128)(2,1)S(1)} %collective-permute-done.24.tail_ref, bf16[768,1024]{1,0:T(8,128)(2,1)S(1)} %get-tuple-element.137.keys_ref, ...), custom_call_target="tpu_custom_call" | custom-call | flops 1024 | bytes 1024 | tf_op jit(solution)/shard_map/forward_conv/pallas_call | solution.py:109
  394.5 17.2 %project.5 = (bf16[2,768,256]{2,1,0:T(8,128)(2,1)S(1)}, bf16[2,768,256]{2,1,0:T(8,128)(2,1)S(1)}) custom-call(bf16[768,1024]{1,0:T(8,128)(2,1)S(1)} %copy-done.2, bf16[768,1024]{1,0:T(8,128)(2,1)} %get-tuple-element.107.refs_1_, bf16[768,1024]{1,0:T(8,128)(2,1)} %get-tuple-element.108.refs_2_, bf16[768,1024]{1,0:T(8,128)(2,1)} %get-tuple-element.109.refs_3_, ...), custom_call_target="tpu_custom_call" | custom-call | flops 1024 | bytes 1024 | tf_op jit(solution)/shard_map/project/pallas_call | solution.py:217
  411.8 5.4 %collective-permute-start.33 = (bf16[2,768,256]{2,1,0:T(8,128)(2,1)S(1)}, bf16[2,768,256]{2,1,0:T(8,128)(2,1)S(1)}, u32[]{:S(2)}, u32[]{:S(2)}) collective-permute-start(bf16[2,768,256]{2,1,0:T(8,128)(2,1)S(1)} %broadcast_select_fusion.8), channel_id=1, source_target_pairs={{0,2},{2,0},{1,3},{3,1},{4,6},{6,4},{5,7},{7,5},{8,10},{10,8},{9,1... | collective-permute-start | bytes 2359304 | tf_op jit(solution)/shard_map/ppermute | solution.py:443
  417.2 23.0 %project.4 = (bf16[3,768,256]{2,1,0:T(8,128)(2,1)S(1)}, bf16[3,768,256]{2,1,0:T(8,128)(2,1)S(1)}) custom-call(bf16[768,1024]{1,0:T(8,128)(2,1)S(1)} %copy-done.2, bf16[768,1024]{1,0:T(8,128)(2,1)} %get-tuple-element.107.refs_1_, bf16[768,1024]{1,0:T(8,128)(2,1)} %get-tuple-element.108.refs_2_, bf16[768,1024]{1,0:T(8,128)(2,1)} %get-tuple-element.109.refs_3_, ...), custom_call_target="tpu_custom_call" | custom-call | flops 1024 | bytes 1024 | tf_op jit(solution)/shard_map/project/pallas_call | solution.py:217
  446.5 17.5 %project.6 = (bf16[2,768,256]{2,1,0:T(8,128)(2,1)S(1)}, bf16[2,768,256]{2,1,0:T(8,128)(2,1)S(1)}) custom-call(bf16[768,1024]{1,0:T(8,128)(2,1)S(1)} %copy-done.2, bf16[768,1024]{1,0:T(8,128)(2,1)} %get-tuple-element.107.refs_1_, bf16[768,1024]{1,0:T(8,128)(2,1)} %get-tuple-element.108.refs_2_, bf16[768,1024]{1,0:T(8,128)(2,1)} %get-tuple-element.109.refs_3_, ...), custom_call_target="tpu_custom_call" | custom-call | flops 1024 | bytes 1024 | tf_op jit(solution)/shard_map/project/pallas_call | solution.py:217
  471.0 13.9 %collective-permute-done.36 = bf16[2,768,256]{2,1,0:T(8,128)(2,1)S(1)} collective-permute-done((bf16[2,768,256]{2,1,0:T(8,128)(2,1)S(1)}, bf16[2,768,256]{2,1,0:T(8,128)(2,1)S(1)}, u32[]{:S(2)}, u32[]{:S(2)}) %collective-permute-start.36) | collective-permute-done | bytes 786464 | tf_op jit(solution)/shard_map/ppermute | solution.py:443
  487.4 12.1 %project.7 = (bf16[1,768,256]{2,1,0:T(8,128)(2,1)S(1)}, bf16[1,768,256]{2,1,0:T(8,128)(2,1)S(1)}) custom-call(bf16[768,1024]{1,0:T(8,128)(2,1)S(1)} %copy-done.2, bf16[768,1024]{1,0:T(8,128)(2,1)} %get-tuple-element.107.refs_1_, bf16[768,1024]{1,0:T(8,128)(2,1)} %get-tuple-element.108.refs_2_, bf16[768,1024]{1,0:T(8,128)(2,1)} %get-tuple-element.109.refs_3_, ...), custom_call_target="tpu_custom_call" | custom-call | flops 1024 | bytes 1024 | tf_op jit(solution)/shard_map/project/pallas_call | solution.py:217
  504.2 7.9 %collective-permute-done.37 = bf16[1,768,256]{2,1,0:T(8,128)(2,1)} collective-permute-done((bf16[1,768,256]{2,1,0:T(8,128)(2,1)}, bf16[1,768,256]{2,1,0:T(8,128)(2,1)}, u32[]{:S(2)}, u32[]{:S(2)}) %collective-permute-start.37) | collective-permute-done | bytes 393248 | tf_op jit(solution)/shard_map/ppermute | solution.py:443
  519.2 7.3 %pick.1 = (bf16[768,2048]{1,0:T(8,128)(2,1)S(1)}, f32[768,1]{1,0:T(8,128)S(1)}) custom-call(s32[3,8]{1,0:T(4,128)S(1)} %pad_add_fusion.1.at_ref, bf16[8,768,256]{2,1,0:T(8,128)(2,1)} %pad_maximum_fusion.2.own_ref, bf16[8,768,256]{2,1,0:T(8,128)(2,1)} %pad_maximum_fusion.3.sib_ref, bf16[768,2048]{1,0:T(8,128)(2,1)} %input_ref.1, ...), custom_call_target="tpu_custom_call" | custom-call | flops 1024 | bytes 1024 | tf_op jit(solution)/shard_map/pick/pallas_call | solution.py:257
  529.5 5.5 %fusion.4 = bf16[768,2048]{1,0:T(8,128)(2,1)} fusion(bf16[768,2048]{1,0:T(8,128)(2,1)} %input_ref.1, bf16[768,2048]{1,0:T(8,128)(2,1)S(1)} %get-tuple-element.127, bf16[768,2048]{1,0:T(8,128)(2,1)} %param.13, f32[768]{0:T(1024)S(1)} %get-tuple-element.131, f32[768]{0:T(1024)S(1)} %get-tuple-element.130, f32[2048]{0:T(1024)S(1)} %convert_element_type.91, ...), kind=kLoop, calls=%fused_computation.9 | loop fusion | flops 17301504 | bytes 12600320 | tf_op jit(solution)/shard_map/convert_element_type | solution.py:483
  (200 shorter events, 118.4 us)
Async XLA Ops:
  0.0 49.0 %collective-permute-start = (bf16[2048,256]{1,0:T(8,128)(2,1)}, bf16[2048,256]{1,0:T(8,128)(2,1)}, u32[]{:S(2)}, u32[]{:S(2)}) collective-permute-start(bf16[2048,256]{1,0:T(8,128)(2,1)} %param.22), channel_id=1, source_target_pairs={{1,2},{2,1},{5,6},{6,5},{9,10},{10,9},{13,14},{14,13},{17,18},{18,... | collective-permute-start | bytes 3145736 | tf_op jit(solution)/shard_map/ppermute | solution.py:312
  1.8 46.4 %collective-permute-start.1 = (bf16[128,128]{1,0:T(8,128)(2,1)}, bf16[128,128]{1,0:T(8,128)(2,1)S(1)}, u32[]{:S(2)}, u32[]{:S(2)}) collective-permute-start(bf16[128,128]{1,0:T(8,128)(2,1)} %param.19), channel_id=1, source_target_pairs={{1,2},{2,1},{5,6},{6,5},{9,10},{10,9},{13,14},{14,13},{17,18},{18,... | collective-permute-start | bytes 98312 | tf_op jit(solution)/shard_map/ppermute | solution.py:312
  51.3 52.7 %collective-permute-start.6 = (bf16[3,256,2048]{2,1,0:T(8,128)(2,1)}, bf16[3,256,2048]{2,1,0:T(8,128)(2,1)}, u32[]{:S(2)}, u32[]{:S(2)}) collective-permute-start(bf16[3,256,2048]{2,1,0:T(8,128)(2,1)} %bitcast.63), channel_id=1, source_target_pairs={{1,2},{2,1},{5,6},{6,5},{9,10},{10,9},{13,14},{14,13},{17,18},{18,... | collective-permute-start | bytes 9437192 | tf_op jit(solution)/shard_map/ppermute | solution.py:312
  104.1 43.3 %collective-permute-start.11 = (bf16[768,2048]{1,0:T(8,128)(2,1)}, bf16[768,2048]{1,0:T(8,128)(2,1)S(1)}, u32[]{:S(2)}, u32[]{:S(2)}) collective-permute-start(bf16[768,2048]{1,0:T(8,128)(2,1)} %param.13), channel_id=1, source_target_pairs={{1,2},{2,1},{5,6},{6,5},{9,10},{10,9},{13,14},{14,13},{17,18},{18,... | collective-permute-start | bytes 9437192 | tf_op jit(solution)/shard_map/ppermute | solution.py:312
  107.3 25.7 %collective-permute-start.7 = (bf16[2048,256]{1,0:T(8,128)(2,1)S(1)}, bf16[2048,256]{1,0:T(8,128)(2,1)S(1)}, u32[]{:S(2)}, u32[]{:S(2)}) collective-permute-start(bf16[2048,256]{1,0:T(8,128)(2,1)S(1)} %collective-permute-done.4), channel_id=1, source_target_pairs={{0,8},{8,16},{16,24},{24,28},{28,20},{20,12},{12,4},{4,0},{1,9},{9... | collective-permute-start | bytes 3145736 | tf_op jit(solution)/shard_map/ppermute | solution.py:321
  147.4 44.4 %collective-permute-start.15 = (bf16[8,2048,256]{2,1,0:T(8,128)(2,1)}, bf16[8,2048,256]{2,1,0:T(8,128)(2,1)}, u32[]{:S(2)}, u32[]{:S(2)}) collective-permute-start(bf16[8,2048,256]{2,1,0:T(8,128)(2,1)} %fusion.5.refs_4_), channel_id=1, source_target_pairs={{0,1},{1,0},{2,3},{3,2},{4,5},{5,4},{6,7},{7,6},{8,9},{9,8},{10,11... | collective-permute-start | bytes 25165832 | tf_op jit(solution)/shard_map/ppermute | solution.py:318
  147.4 34.8 %collective-permute-start.14 = (bf16[768,2048]{1,0:T(8,128)(2,1)S(1)}, bf16[768,2048]{1,0:T(8,128)(2,1)S(1)}, u32[]{:S(2)}, u32[]{:S(2)}) collective-permute-start(bf16[768,2048]{1,0:T(8,128)(2,1)S(1)} %copy-done.13), channel_id=1, source_target_pairs={{0,2},{1,0},{2,3},{3,1},{4,6},{5,4},{6,7},{7,5},{8,10},{9,8},{10,1... | collective-permute-start | bytes 9437192 | tf_op jit(solution)/shard_map/ppermute | solution.py:386
  147.4 70.6 %collective-permute-start.12 = (bf16[3,256,2048]{2,1,0:T(8,128)(2,1)S(1)}, bf16[3,256,2048]{2,1,0:T(8,128)(2,1)}, u32[]{:S(2)}, u32[]{:S(2)}) collective-permute-start(bf16[3,256,2048]{2,1,0:T(8,128)(2,1)S(1)} %broadcast_select_fusion.3.refs_10_), channel_id=1, source_target_pairs={{0,8},{8,16},{16,24},{24,28},{28,20},{20,12},{12,4},{4,0},{1,9},{9... | collective-permute-start | bytes 9437192 | tf_op jit(solution)/shard_map/ppermute | solution.py:321
  149.4 70.3 %collective-permute-start.13 = (bf16[3,256,2048]{2,1,0:T(8,128)(2,1)S(1)}, bf16[3,256,2048]{2,1,0:T(8,128)(2,1)}, u32[]{:S(2)}, u32[]{:S(2)}) collective-permute-start(bf16[3,256,2048]{2,1,0:T(8,128)(2,1)S(1)} %broadcast_select_fusion.3.refs_10_), channel_id=1, source_target_pairs={{8,0},{16,8},{24,16},{28,24},{20,28},{12,20},{4,12},{0,4},{9,1},{1... | collective-permute-start | bytes 9437192 | tf_op jit(solution)/shard_map/ppermute | solution.py:321
  183.9 35.8 %collective-permute-start.16 = (bf16[768,2048]{1,0:T(8,128)(2,1)}, bf16[768,2048]{1,0:T(8,128)(2,1)}, u32[]{:S(2)}, u32[]{:S(2)}) collective-permute-start(bf16[768,2048]{1,0:T(8,128)(2,1)} %param.17), channel_id=1, source_target_pairs={{1,2},{2,1},{5,6},{6,5},{9,10},{10,9},{13,14},{14,13},{17,18},{18,... | collective-permute-start | bytes 9437192 | tf_op jit(solution)/shard_map/ppermute | solution.py:312
  220.5 138.8 %collective-permute-start.17 = (bf16[3,256,2048]{2,1,0:T(8,128)(2,1)}, bf16[3,256,2048]{2,1,0:T(8,128)(2,1)}, u32[]{:S(2)}, u32[]{:S(2)}) collective-permute-start(bf16[3,256,2048]{2,1,0:T(8,128)(2,1)} %collective-permute-done.12.refs_11_), channel_id=1, source_target_pairs={{0,8},{8,16},{16,24},{24,28},{28,20},{20,12},{12,4},{4,0},{1,9},{9... | collective-permute-start | bytes 9437192 | tf_op jit(solution)/shard_map/ppermute | solution.py:321
  222.3 137.1 %collective-permute-start.18 = (bf16[3,256,2048]{2,1,0:T(8,128)(2,1)}, bf16[3,256,2048]{2,1,0:T(8,128)(2,1)}, u32[]{:S(2)}, u32[]{:S(2)}) collective-permute-start(bf16[3,256,2048]{2,1,0:T(8,128)(2,1)} %collective-permute-done.13.refs_12_), channel_id=1, source_target_pairs={{8,0},{16,8},{24,16},{28,24},{20,28},{12,20},{4,12},{0,4},{9,1},{1... | collective-permute-start | bytes 9437192 | tf_op jit(solution)/shard_map/ppermute | solution.py:321
  222.8 73.7 %collective-permute-start.20 = (bf16[768,1024]{1,0:T(8,128)(2,1)S(1)}, bf16[768,1024]{1,0:T(8,128)(2,1)}, u32[]{:S(2)}, u32[]{:S(2)}) collective-permute-start(bf16[768,1024]{1,0:T(8,128)(2,1)S(1)} %slice.82), channel_id=1, source_target_pairs={{1,2},{2,1},{5,6},{6,5},{9,10},{10,9},{13,14},{14,13},{17,18},{18,... | collective-permute-start | bytes 4718600 | tf_op jit(solution)/shard_map/ppermute | solution.py:312
  227.2 45.1 %collective-permute-start.21 = (bf16[128,2048]{1,0:T(8,128)(2,1)S(1)}, bf16[128,2048]{1,0:T(8,128)(2,1)S(1)}, u32[]{:S(2)}, u32[]{:S(2)}) collective-permute-start(bf16[128,2048]{1,0:T(8,128)(2,1)S(1)} %multiply_convert_fusion), channel_id=1, source_target_pairs={{1,0},{4,1},{5,4},{8,5},{9,8},{12,9},{13,12},{16,13},{17,16},{20,1... | collective-permute-start | bytes 1572872 | tf_op jit(solution)/shard_map/ppermute | solution.py:406
  298.6 60.8 %collective-permute-start.23 = (bf16[768,1024]{1,0:T(8,128)(2,1)}, bf16[768,1024]{1,0:T(8,128)(2,1)}, u32[]{:S(2)}, u32[]{:S(2)}) collective-permute-start(bf16[768,1024]{1,0:T(8,128)(2,1)} %get-tuple-element.139), channel_id=1, source_target_pairs={{1,2},{2,1},{5,6},{6,5},{9,10},{10,9},{13,14},{14,13},{17,18},{18,... | collective-permute-start | bytes 4718600 | tf_op jit(solution)/shard_map/ppermute | solution.py:312
  300.6 86.4 %collective-permute-start.29 = (bf16[768,2048]{1,0:T(8,128)(2,1)S(1)}, bf16[768,2048]{1,0:T(8,128)(2,1)}, u32[]{:S(2)}, u32[]{:S(2)}) collective-permute-start(bf16[768,2048]{1,0:T(8,128)(2,1)S(1)} %get-tuple-element.110.refs_4_), channel_id=1, source_target_pairs={{0,1},{1,0},{2,3},{3,2},{4,5},{5,4},{6,7},{7,6},{8,9},{9,8},{10,11... | collective-permute-start | bytes 9437192 | tf_op jit(solution)/shard_map/ppermute | solution.py:318
  359.4 27.7 %collective-permute-start.25 = (bf16[768,1024]{1,0:T(8,128)(2,1)S(1)}, bf16[768,1024]{1,0:T(8,128)(2,1)S(1)}, u32[]{:S(2)}, u32[]{:S(2)}) collective-permute-start(bf16[768,1024]{1,0:T(8,128)(2,1)S(1)} %get-tuple-element.105.refs_0_), channel_id=1, source_target_pairs={{0,1},{1,0},{2,3},{3,2},{4,5},{5,4},{6,7},{7,6},{8,9},{9,8},{10,11... | collective-permute-start | bytes 4718600 | tf_op jit(solution)/shard_map/ppermute | solution.py:318
  368.0 72.7 %collective-permute-start.31 = (bf16[3,256,2048]{2,1,0:T(8,128)(2,1)}, bf16[3,256,2048]{2,1,0:T(8,128)(2,1)}, u32[]{:S(2)}, u32[]{:S(2)}) collective-permute-start(bf16[3,256,2048]{2,1,0:T(8,128)(2,1)} %collective-permute-done.17.refs_10_), channel_id=1, source_target_pairs={{0,8},{8,16},{16,24},{24,28},{28,20},{20,12},{12,4},{4,0},{1,9},{9... | collective-permute-start | bytes 9437192 | tf_op jit(solution)/shard_map/ppermute | solution.py:321
  369.8 70.9 %collective-permute-start.32 = (bf16[3,256,2048]{2,1,0:T(8,128)(2,1)}, bf16[3,256,2048]{2,1,0:T(8,128)(2,1)}, u32[]{:S(2)}, u32[]{:S(2)}) collective-permute-start(bf16[3,256,2048]{2,1,0:T(8,128)(2,1)} %collective-permute-done.18.refs_11_), channel_id=1, source_target_pairs={{8,0},{16,8},{24,16},{28,24},{20,28},{12,20},{4,12},{0,4},{9,1},{1... | collective-permute-start | bytes 9437192 | tf_op jit(solution)/shard_map/ppermute | solution.py:321
  411.8 28.7 %collective-permute-start.33 = (bf16[2,768,256]{2,1,0:T(8,128)(2,1)S(1)}, bf16[2,768,256]{2,1,0:T(8,128)(2,1)S(1)}, u32[]{:S(2)}, u32[]{:S(2)}) collective-permute-start(bf16[2,768,256]{2,1,0:T(8,128)(2,1)S(1)} %broadcast_select_fusion.8), channel_id=1, source_target_pairs={{0,2},{2,0},{1,3},{3,1},{4,6},{6,4},{5,7},{7,5},{8,10},{10,8},{9,1... | collective-permute-start | bytes 2359304 | tf_op jit(solution)/shard_map/ppermute | solution.py:443
  440.3 29.0 %collective-permute-start.30 = (bf16[3,768,256]{2,1,0:T(8,128)(2,1)S(1)}, bf16[3,768,256]{2,1,0:T(8,128)(2,1)}, u32[]{:S(2)}, u32[]{:S(2)}) collective-permute-start(bf16[3,768,256]{2,1,0:T(8,128)(2,1)S(1)} %broadcast_select_fusion.5), channel_id=1, source_target_pairs={{0,2},{2,0},{1,3},{3,1},{4,6},{6,4},{5,7},{7,5},{8,10},{10,8},{9,1... | collective-permute-start | bytes 3538952 | tf_op jit(solution)/shard_map/ppermute | solution.py:443
  442.3 42.9 %collective-permute-start.34 = (bf16[3,128,2048]{2,1,0:T(8,128)(2,1)S(1)}, bf16[3,128,2048]{2,1,0:T(8,128)(2,1)S(1)}, u32[]{:S(2)}, u32[]{:S(2)}) collective-permute-start(bf16[3,128,2048]{2,1,0:T(8,128)(2,1)S(1)} %slice.97), channel_id=1, source_target_pairs={{0,8},{8,16},{16,24},{24,28},{28,20},{20,12},{12,4},{4,0},{1,9},{9... | collective-permute-start | bytes 4718600 | tf_op jit(solution)/shard_map/ppermute | solution.py:321
  446.4 38.8 %collective-permute-start.35 = (bf16[3,128,2048]{2,1,0:T(8,128)(2,1)S(1)}, bf16[3,128,2048]{2,1,0:T(8,128)(2,1)S(1)}, u32[]{:S(2)}, u32[]{:S(2)}) collective-permute-start(bf16[3,128,2048]{2,1,0:T(8,128)(2,1)S(1)} %slice.98), channel_id=1, source_target_pairs={{8,0},{16,8},{24,16},{28,24},{20,28},{12,20},{4,12},{0,4},{9,1},{1... | collective-permute-start | bytes 4718600 | tf_op jit(solution)/shard_map/ppermute | solution.py:321
  487.4 28.7 %collective-permute-start.38 = (bf16[3,768,256]{2,1,0:T(8,128)(2,1)S(1)}, bf16[3,768,256]{2,1,0:T(8,128)(2,1)}, u32[]{:S(2)}, u32[]{:S(2)}) collective-permute-start(bf16[3,768,256]{2,1,0:T(8,128)(2,1)S(1)} %add_convert_fusion), channel_id=1, source_target_pairs={{0,1},{1,0},{2,3},{3,2},{4,5},{5,4},{6,7},{7,6},{8,9},{9,8},{10,11... | collective-permute-start | bytes 3538952 | tf_op jit(solution)/shard_map/ppermute | solution.py:469
  (44 other events, 672.1 us)
where the time goes:
time: 545 us; the launch traced here: 535 us
  waiting for transfers between devices  173 us (32%)
  Pallas kernels  155 us (28%)
  starting transfers between devices  78.4 us (14%)
  blocking collectives  48.4 us (9%)
  other arithmetic  41.4 us (8%)
  local copies, waits for them, and re-layouts  37.3 us (7%)
    ppermute x16, waiting for transfers between devices, both_ways(): return (lax.ppermute(up, ('o',), forth), lax.ppermute(down, ('o',), back))  71 us
    pallas_call x4, Pallas kernels, project(): pl.pallas_call(functools.partial(project_kernel, places, blocks), grid=(2...  69.8 us
    pallas_call x3, Pallas kernels, conv_call(): pl.pallas_call(functools.partial(kernel, taps, per), grid=(width // cols,...  54.3 us
    all_gather x1, blocking collectives, on_device(): all_starts = lax.all_gather(doc_starts, ('o', 'x'), axis=0, tiled=True)  45.7 us
    ppermute x1, waiting for transfers between devices, on_device(): head = lax.ppermute(head, ('o', 'c'), backward)  39.9 us
    ppermute x1, waiting for transfers between devices, on_device(): grad_other = lax.ppermute(grad_out, ('x', 'c'), CYCLE)  32.7 us
    ppermute x6, starting transfers between devices, sibling(): return lax.ppermute(block, 'c', PAIR)  32.6 us
    ppermute x4, waiting for transfers between devices, add_blocks(): received = lax.ppermute(send, 'x', PAIR)  25 us
  transfers between devices with their start and end apart: 42, of which 14 were waited for; matrix products, arithmetic and copies ran while one was open for 11% of the time, Pallas kernels for 28%

commit v1 on v0

--- a/solution.py
+++ b/solution.py
@@ -10,7 +10,7 @@
 
 LANES = 128
 EPSILON = 1e-05
-VMEM_BYTES = 48 * 1024 * 1024
+VMEM_BYTES = 52 * 1024 * 1024
 
 BRIEF = pl.CostEstimate(flops=1024, bytes_accessed=1024, transcendentals=0)
 
@@ -76,14 +76,13 @@
 
 
 def backward_kernel(
-    taps, count, base_ref, last_ref, head_ref, keys_ref, queries_ref, mix_ref,
+    taps, count, base_ref, last_ref, keys_ref, queries_ref, mix_ref,
     conv_ref, v_ref, table_ref, source_ref,
 ):
     rows, width = keys_ref.shape
     parts = width // LANES
     toeplitz_into(table_ref, base_ref, taps, parts * count)
     source_ref[:rows, :] = (mix_ref[...] * queries_ref[...].astype(jnp.float32)).astype(jnp.bfloat16)
-    source_ref[rows:, :] = head_ref[...]
 
     def tile(i, carry):
         row = pl.multiple_of(i * taps, taps)
@@ -98,24 +97,53 @@
             v_ref[at] = (conv * keys_ref[at].astype(jnp.float32)).astype(v_ref.dtype)
         return carry
 
-    lax.fori_loop(0, rows // taps, tile, 0)
-
-
-def conv_call(kernel, name, base, last, edge, operands, dtypes, taps, per):
-    rows, width = operands[0].shape
+    lax.fori_loop(0, rows // taps - 1, tile, 0)
+
+
+def ending_kernel(
+    taps, count, base_ref, last_ref, head_ref, keys_ref, queries_ref, mix_ref, conv_in, v_in,
+    conv_ref, v_ref, table_ref,
+):
+    del conv_in, v_in
+    rows = last_ref.shape[1] - taps
+    parts = keys_ref.shape[1] // LANES
+    toeplitz_into(table_ref, base_ref, taps, parts * count)
+    current = (mix_ref[...] * queries_ref[...].astype(jnp.float32)).astype(jnp.bfloat16)
+    source = jnp.concatenate([current, head_ref[...]], axis=0)
+    at_row = lax.broadcasted_iota(jnp.int32, (taps, 2 * taps), 0) + rows - taps
+    keep = jnp.where(at_row >= last_ref[:, rows - taps :], 1.0, 0.0).astype(jnp.bfloat16)
+    for p in range(parts):
+        lanes = slice(p * LANES, (p + 1) * LANES)
+        table = table_ref[p * count * taps : (p + 1) * count * taps, :]
+        conv = banded(table, keep, source[:, lanes], taps, count)
+        conv_ref[:, lanes] = conv
+        v_ref[:, lanes] = (conv * keys_ref[:, lanes].astype(jnp.float32)).astype(v_ref.dtype)
+
+
+def conv_call(kernel, name, base, last, edge, operands, dtypes, taps, per, width, start=0):
+    rows = operands[0].shape[0]
     cols = min(width, 4 * LANES)
     count = cols // LANES * per
-    slab = pl.BlockSpec((rows, cols), lambda g: (0, g))
+    skip = start // cols
+
+    def offset(whole):
+        return skip if whole != width else 0
+
+    edges = [] if edge is None else [edge]
+    ahead = skip
     return pl.pallas_call(
         functools.partial(kernel, taps, per),
         grid=(width // cols,),
         in_specs=[
-            pl.BlockSpec((count, 2 * taps), lambda g: (g, 0)),
+            pl.BlockSpec((count, 2 * taps), lambda g: (g + ahead, 0)),
             pl.BlockSpec(last.shape, lambda g: (0, 0)),
-            pl.BlockSpec((taps, cols), lambda g: (0, g)),
         ]
-        + [slab] * len(operands),
-        out_specs=[slab] * len(dtypes),
+        + [pl.BlockSpec((taps, cols), lambda g: (0, g + ahead))] * len(edges)
+        + [
+            pl.BlockSpec((rows, cols), lambda g, d=offset(operand.shape[1]): (0, g + d))
+            for operand in operands
+        ],
+        out_specs=[pl.BlockSpec((rows, cols), lambda g: (0, g))] * len(dtypes),
         out_shape=[jax.ShapeDtypeStruct((rows, width), t) for t in dtypes],
         scratch_shapes=[
             pltpu.VMEM((count * taps, 2 * taps), jnp.bfloat16),
@@ -124,7 +152,32 @@
         compiler_params=params(1),
         cost_estimate=BRIEF,
         name=name,
-    )(base, last, edge, *operands)
+    )(base, last, *edges, *operands)
+
+
+def ending_call(base, last, head, operands, conv, grad, taps, per):
+    rows, width = conv.shape
+    cols = min(width, 4 * LANES)
+    count = cols // LANES * per
+    tile = pl.BlockSpec((taps, cols), lambda g: (rows // taps - 1, g))
+    whole = pl.BlockSpec(memory_space=pl.ANY)
+    return pl.pallas_call(
+        functools.partial(ending_kernel, taps, per),
+        grid=(width // cols,),
+        in_specs=[
+            pl.BlockSpec((count, 2 * taps), lambda g: (g, 0)),
+            pl.BlockSpec(last.shape, lambda g: (0, 0)),
+            pl.BlockSpec((taps, cols), lambda g: (0, g)),
+            tile, tile, tile, whole, whole,
+        ],
+        out_specs=[tile, tile],
+        out_shape=[jax.ShapeDtypeStruct(a.shape, a.dtype) for a in (conv, grad)],
+        scratch_shapes=[pltpu.VMEM((count * taps, 2 * taps), jnp.bfloat16)],
+        input_output_aliases={6: 0, 7: 1},
+        compiler_params=params(1),
+        cost_estimate=BRIEF,
+        name="backward_ending",
+    )(base, last, head, *operands, conv, grad)
 
 
 NT = (((1,), (1,)), ((), ()))
@@ -219,7 +272,10 @@
         grid=(2 * half,),
         in_specs=[pl.BlockSpec((step, p.shape[1]), lambda i: (first(i), 0)) for p in own]
         + [pl.BlockSpec((step, p.shape[1]), lambda i: (second(i), 0)) for p in sib]
-        + [pl.BlockSpec((branches, feats, width), lambda i: (0, 0, 0))] * blocks,
+        + [
+            pl.BlockSpec((branches, feats, width), lambda i: (0, 0, 0), pipeline_mode=pl.Buffered(1))
+        ]
+        * blocks,
         out_specs=[
             pl.BlockSpec((blocks, step, feats), lambda i: (0, first(i), 0)),
             pl.BlockSpec((blocks, step, feats), lambda i: (0, second(i), 0)),
@@ -327,22 +383,43 @@
             lax.slice_in_dim(down, half, 2 * half, axis=axis),
         )
 
-    all_starts = lax.all_gather(doc_starts, ("o", "x"), axis=0, tiled=True)
+    def neighbour(block, distance):
+        route = []
+        for i in range(count):
+            for core in range(2):
+                source = i * 2 + core + distance
+                if 0 <= source < 2 * count:
+                    route += [(source * 2 + side, (i * 2 + side) * 2 + core) for side in range(2)]
+        return lax.ppermute(block, ("o", "x", "c"), route)
+
+    starts = swapped(doc_starts)[0]
+    prior = neighbour(doc_starts, -1)[0, -1]
+    following = neighbour(doc_starts, 1)[0]
+    tail = (keys[rows - taps :].astype(jnp.float32) * values[rows - taps :].astype(jnp.float32)).astype(
+        jnp.bfloat16
+    )
     taps32 = swapped(filters).astype(jnp.float32)
     out_w = swapped(out_weight)
     in_w = jnp.swapaxes(in_weight, 0, 1)
-    out_w, in_w, grad_out, taps32 = fence(out_w, in_w, grad_out, taps32)
-
-    in_recv = exchanged(in_w)
+    out_w, in_w, grad_out, taps32, starts, prior, following, tail = fence(
+        out_w, in_w, grad_out, taps32, starts, prior, following, tail
+    )
+
+    in_recv, half_recv = exchanged(in_w), exchanged(grad_out)
+    tail = neighbour(tail, -1)
     blocks = [out_w]
     up = down = out_w
     for s in range(1, far):
         up, down = both_ways(up, down)
-        if s == far - 2:
-            up, down, in_recv, in_w, grad_out = fence(up, down, in_recv, in_w, grad_out)
+        if s == far - 1:
+            up, down, in_recv, in_w, half_recv, grad_out, tail = fence(
+                up, down, in_recv, in_w, half_recv, grad_out, tail
+            )
         blocks += [up, down]
     in_w = jnp.where(x == c, in_w, in_recv)
-    half_recv = exchanged(grad_out)
+    spans = (slice(0, rows // 2), slice(rows // 2, rows))
+    other_up = lax.ppermute(grad_out[spans[0]], ("x", "c"), CYCLE)
+    grad_half = jnp.where(x == c, grad_out, half_recv)
     blocks.append(jnp.concatenate(far_halves(up, down, 0), axis=0))
     own_out = jnp.stack(blocks)
     source_in = block_input.astype(jnp.float32)
@@ -359,103 +436,113 @@
 
     columns = jnp.stack([column(c), column(1 - c)])
     slabs = 2 * count
-    slab = o * 2 + c
-    onward = [(i, i + 1) for i in range(slabs - 1)]
     backward = [(i + 1, i) for i in range(slabs - 1)]
     positions = jnp.arange(rows, dtype=jnp.int32)
 
-    def last_of(at):
-        starts = all_starts[jnp.minimum(at, slabs - 1)]
-        prior = jnp.where(at > 0, all_starts[jnp.maximum(at - 1, 0), -1], 0)
-        own = jnp.where(starts[None, :] <= positions[:, None], starts[None, :], -rows)
-        return jnp.maximum(jnp.max(own, axis=1), prior - rows)
-
-    last_start = last_of(slab)
-    padded_last = jnp.concatenate([last_start, last_of(slab + 1)[:taps] + rows])[None]
+    def last_of(own, before):
+        own = jnp.where(own[None, :] <= positions[:, None], own[None, :], -rows)
+        return jnp.maximum(jnp.max(own, axis=1), before - rows)
+
+    last_start = last_of(starts, prior)
+    padded_last = jnp.concatenate([last_start, last_of(following, starts[-1])[:taps] + rows])[None]
     edge = jnp.zeros((groups, taps), jnp.float32)
     base_back = jnp.concatenate([taps32, edge], axis=1)
     base_fore = jnp.concatenate([edge[:, :1], taps32[:, ::-1], edge[:, 1:]], axis=1)
-    own_out, in_w, half_recv, grad_out, square_sum, padded_last, last_col, base_back, base_fore, columns = fence(
-        own_out, in_w, half_recv, grad_out, square_sum, padded_last, last_start[:, None], base_back,
+    (
+        own_out, in_w, grad_half, grad_out, other_up, square_sum, padded_last, last_col, base_back, base_fore,
+        columns,
+    ) = fence(
+        own_out, in_w, grad_half, grad_out, other_up, square_sum, padded_last, last_start[:, None], base_back,
         base_fore, columns,
     )
 
     ahead, behind = {0: in_w}, {0: in_w}
     ahead[1], behind[1] = both_ways(in_w, in_w)
     sib_out = sibling(own_out)
-    grad_other = lax.ppermute(grad_out, ("x", "c"), CYCLE)
-    grad_other, keys = fence(grad_other, keys)
-    k_recv = exchanged(keys)
-    grad_half = jnp.where(x == c, grad_out, half_recv)
+    other_down = lax.ppermute(grad_out[spans[1]], ("x", "c"), CYCLE)
+    grad_other = jnp.concatenate([other_up, other_down], axis=0)
+    k_recv, q_recv = exchanged(keys), [exchanged(queries[spans[0]])]
     if n_chan > 1:
         grad_half = lax.all_gather(grad_half, "h", axis=1, tiled=True)
         grad_other = lax.all_gather(grad_other, "h", axis=1, tiled=True)
     grads = jnp.concatenate([grad_half, grad_other], axis=1)
     mix_grad = mix_matmul(columns, grads, own_out, sib_out)
-    ahead[1], behind[1], mix_grad, k_recv, queries = fence(
-        ahead[1], behind[1], mix_grad, k_recv, queries
+    ahead[1], behind[1], mix_grad, k_recv, keys, q_recv[0], queries = fence(
+        ahead[1], behind[1], mix_grad, k_recv, keys, q_recv[0], queries
     )
 
     ahead[2], behind[2] = both_ways(ahead[1], behind[1])
-    q_recv, queries, values, mix_grad = fence(exchanged(queries), queries, values, mix_grad)
+    q_recv.append(exchanged(queries[spans[1]]))
+    q_recv[1], queries, values, mix_grad = fence(q_recv[1], queries, values, mix_grad)
     middle = width // 2
     parts = (slice(0, middle), slice(middle, width))
-    v_recv = exchanged(values[:, parts[0]])
-    own_k, own_q = jnp.where(x == c, keys, k_recv), jnp.where(x == c, queries, q_recv)
+    v_recv = [exchanged(values[:, part]) for part in parts]
+    own_k = jnp.where(x == c, keys, k_recv)
+    own_q = jnp.where(x == c, queries, jnp.concatenate(q_recv, axis=0))
     head = (mix_grad[:taps] * own_q[:taps].astype(jnp.float32)).astype(jnp.bfloat16)
     head = lax.ppermute(head, ("o", "c"), backward)
     conv, v_grad = conv_call(
-        backward_kernel, "backward_conv", base_back, padded_last, head,
-        [own_k, own_q, mix_grad], [jnp.float32, jnp.bfloat16], taps, per,
-    )
-    v_recv, values, conv, v_grad = fence(v_recv, values, conv, v_grad)
-
-    def forward(at, received):
-        own_v = jnp.where(x == c, values[:, parts[at]], received)
-        part_k = own_k[:, parts[at]]
-        tail = part_k[rows - taps :].astype(jnp.float32) * own_v[rows - taps :].astype(jnp.float32)
-        tail = lax.ppermute(tail.astype(jnp.bfloat16), ("o", "c"), onward)
-        base = base_fore[at * groups // 2 : (at + 1) * groups // 2]
+        backward_kernel, "backward_conv", base_back, padded_last, None,
+        [own_k, own_q, mix_grad], [jnp.float32, jnp.bfloat16], taps, per, width,
+    )
+    conv, v_grad = ending_call(
+        base_back, padded_last, head, [own_k, own_q, mix_grad], conv, v_grad, taps, per
+    )
+    *v_recv, values, conv, v_grad = fence(*v_recv, values, conv, v_grad)
+
+    def forward(at):
+        own_v = jnp.where(x == c, values[:, parts[at]], v_recv[at])
         return conv_call(
-            forward_kernel, "forward_conv", base, last_col, tail,
-            [part_k, own_v, mix_grad[:, parts[at]], conv[:, parts[at]]],
-            [jnp.bfloat16, jnp.bfloat16], taps, per,
+            forward_kernel, "forward_conv", base_fore, last_col, tail,
+            [own_k, own_v, mix_grad, conv], [jnp.bfloat16, jnp.bfloat16], taps, per, middle, at * middle,
         )
 
-    later = exchanged(values[:, parts[1]])
-    q_left, k_left = forward(0, v_recv)
-    sib_v = sibling(v_grad)
-    ahead[2], behind[2], q_left, k_left, later, v_grad = fence(
-        ahead[2], behind[2], q_left, k_left, later, v_grad
+    q_left, k_left = forward(0)
+    sib_q, sib_k, sib_v = sibling(q_left), sibling(k_left), sibling(v_grad)
+    ahead[2], behind[2], q_left, k_left, v_grad, sib_q, sib_k, sib_v, v_recv[1] = fence(
+        ahead[2], behind[2], q_left, k_left, v_grad, sib_q, sib_k, sib_v, v_recv[1]
     )
 
     ahead[3], behind[3] = both_ways(ahead[2], behind[2])
-    q_right, k_right = forward(1, later)
+    q_right, k_right = forward(1)
     own_grads = [[q_left, q_right], [k_left, k_right], [v_grad]]
-    sib_grads = [[sibling(p) for p in pieces] for pieces in own_grads[:2]] + [[sib_v]]
+    sib_grads = [[sib_q, sibling(q_right)], [sib_k, sibling(k_right)], [sib_v]]
+
+    def partial_sums(weights):
+        ours, theirs = project(own_grads, sib_grads, weights)
+        return jnp.where(c == x, ours, theirs), jnp.where(c == x, theirs, ours)
+
+    def summed(keep, received):
+        return (keep.astype(jnp.float32) + received.astype(jnp.float32)).astype(jnp.bfloat16)
+
+    def over_x(block):
+        return lax.ppermute(block, "x", PAIR)
 
     norms = []
-
-    def add_blocks(weights):
-        ours, theirs = project(own_grads, sib_grads, weights)
-        keep = jnp.where(c == x, ours, theirs)
-        send = jnp.where(c == x, theirs, ours)
-        received = lax.ppermute(send, "x", PAIR)
-        norms.append((keep.astype(jnp.float32) + received.astype(jnp.float32)).astype(jnp.bfloat16))
-
+    ready = [ahead[2], behind[2]]
     for s in range(3, far + 1):
         if 3 < s < far:
             ahead[s], behind[s] = both_ways(ahead[s - 1], behind[s - 1])
         elif s == far:
             up, down = far_halves(ahead[s - 1], behind[s - 1], 1)
-        if s == 3:
-            add_blocks([in_w, ahead[1], behind[1]])
-        add_blocks([ahead[s - 1], behind[s - 1]])
-        if s < far:
-            ahead[s], behind[s], norms[-1] = fence(ahead[s], behind[s], norms[-1])
+        early = partial_sums([in_w, ahead[1], behind[1]]) if s == 3 else None
+        keep, send = partial_sums(ready)
+        if early:
+            first, received = early[0], over_x(early[1])
+            ahead[s], behind[s], first, received, keep, send = fence(
+                ahead[s], behind[s], first, received, keep, send
+            )
+            norms.append(summed(first, received))
+            ready = [ahead[s], behind[s]]
+        elif s < far:
+            ahead[s], behind[s], keep, send = fence(ahead[s], behind[s], keep, send)
+            ready = [ahead[s], behind[s]]
         else:
-            up, down, norms[-1] = fence(up, down, norms[-1])
-    add_blocks([jnp.concatenate([up, down], axis=1)])
+            up, down, keep, send = fence(up, down, keep, send)
+            ready = [jnp.concatenate([up, down], axis=1)]
+        norms.append(summed(keep, over_x(send)))
+    keep, send = partial_sums(ready)
+    norms.append(summed(keep, over_x(send)))
     if n_chan > 1:
         norm = jnp.concatenate(norms, axis=0)
         slot = jnp.zeros((count,), jnp.int32).at[sources].set(jnp.arange(count, dtype=jnp.int32))

time: 545 us -> 505 us (0.927)
  waiting for transfers between devices: 173 us -> 126 us
  blocking collectives: 48.4 us -> 2.66 us
  starting transfers between devices: 78.4 us -> 120 us
  other arithmetic: 41.4 us -> 57.7 us
  local copies, waits for them, and re-layouts: 37.3 us -> 26.4 us
  Pallas kernels: 155 us -> 161 us
    all_gather x1 -> x0, blocking collectives: 45.7 us -> none  [on_device(): all_starts = lax.all_gather(doc_starts, ('o', 'x'), axis=0, tiled=True)]
    ppermute x1, waiting for transfers between devices: 39.9 us -> 0.01 us  [on_device(): head = lax.ppermute(head, ('o', 'c'), backward)]
    ppermute x16, starting transfers between devices: 17.4 us -> 38.6 us  [both_ways(): return (lax.ppermute(up, ('o',), forth), lax.ppermute(down, ('o',), back))]
    ppermute x16, waiting for transfers between devices: 71 us -> 58.5 us  [both_ways(): return (lax.ppermute(up, ('o',), forth), lax.ppermute(down, ('o',), back))]
    ppermute x7 -> x9, starting transfers between devices: 13.8 us -> 25 us  [the longest x3 20.6 us: neighbour(): return lax.ppermute(block, ('o', 'x', 'c'), route)]
    select_n x7 -> x8, other arithmetic: 5.54 us -> 15 us  [the longest x4 4.19 us: partial_sums(): return (jnp.where(c == x, ours, theirs), jnp.where(c == x, theirs, ours))]
    ppermute x6, starting transfers between devices: 32.6 us -> 40.3 us  [sibling(): return lax.ppermute(block, 'c', PAIR)]
    ppermute x6, waiting for transfers between devices: 4.3 us -> 11 us  [sibling(): return lax.ppermute(block, 'c', PAIR)]
  transfers between devices with their start and end apart: 42 -> 46, of which waited for: 14 -> 16; matrix products, arithmetic and copies ran while one was open for 11% -> 14% of each run, Pallas kernels for 28% -> 31%
where the time goes in v1:
time: 505 us; the launch traced here: 496 us
  Pallas kernels  161 us (32%)
  waiting for transfers between devices  126 us (25%)
  starting transfers between devices  120 us (24%)
  other arithmetic  57.7 us (11%)
  local copies, waits for them, and re-layouts  26.4 us (5%)
    pallas_call x4, Pallas kernels, project(): pl.pallas_call(functools.partial(project_kernel, places, blocks), grid=(2...  70.3 us
    ppermute x16, waiting for transfers between devices, both_ways(): return (lax.ppermute(up, ('o',), forth), lax.ppermute(down, ('o',), back))  58.5 us
    pallas_call x3, Pallas kernels, conv_call(): pl.pallas_call(functools.partial(kernel, taps, per), grid=(width // cols,...  52.1 us
    ppermute x6, starting transfers between devices, sibling(): return lax.ppermute(block, 'c', PAIR)  40.3 us
    ppermute x16, starting transfers between devices, both_ways(): return (lax.ppermute(up, ('o',), forth), lax.ppermute(down, ('o',), back))  38.6 us
    ppermute x1, waiting for transfers between devices, on_device(): other_down = lax.ppermute(grad_out[spans[1]], ('x', 'c'), CYCLE)  27 us
    pallas_call x1, Pallas kernels, mix_matmul(): pl.pallas_call(mix_kernel, grid_spec=pltpu.PrefetchScalarGridSpec(num_sca...  23.3 us
    ppermute x3, starting transfers between devices, neighbour(): return lax.ppermute(block, ('o', 'x', 'c'), route)  20.6 us
  transfers between devices with their start and end apart: 46, of which 16 were waited for; matrix products, arithmetic and copies ran while one was open for 14% of the time, Pallas kernels for 31%

profile of v1, /device:TPU:0, one launch (start us, length us, event | category | flops | bytes accessed | tf_op | source)
XLA Modules:
  0.0 496.0 jit_solution(10724271249722641672)
XLA Ops:
  0.8 6.2 %collective-permute-start.3 = (s32[1,4]{1,0:T(1,128)}, s32[1,4]{1,0:T(1,128)S(1)}, u32[]{:S(2)}, u32[]{:S(2)}) collective-permute-start(s32[1,4]{1,0:T(1,128)} %param.20), channel_id=1, source_target_pairs={{0,1},{1,3},{2,4},{3,6},{4,5},{5,7},{6,8},{7,10},{8,9},{9,11},{10,... | collective-permute-start | bytes 56 | tf_op jit(solution)/shard_map/ppermute | solution.py:393
  26.1 13.1 %collective-permute-start.13 = (bf16[128,2048]{1,0:T(8,128)(2,1)S(1)}, bf16[128,2048]{1,0:T(8,128)(2,1)S(1)}, u32[]{:S(2)}, u32[]{:S(2)}) collective-permute-start(bf16[128,2048]{1,0:T(8,128)(2,1)S(1)} %multiply_convert_fusion.1), channel_id=1, source_target_pairs={{0,1},{1,3},{2,4},{3,6},{4,5},{5,7},{6,8},{7,10},{8,9},{9,11},{10,... | collective-permute-start | bytes 1572872 | tf_op jit(solution)/shard_map/ppermute | solution.py:393
  46.8 18.2 %collective-permute-done.8 = bf16[2048,256]{1,0:T(8,128)(2,1)S(1)} collective-permute-done((bf16[2048,256]{1,0:T(8,128)(2,1)S(1)}, bf16[2048,256]{1,0:T(8,128)(2,1)S(1)}, u32[]{:S(2)}, u32[]{:S(2)}) %collective-permute-start.8) | collective-permute-done | bytes 1048608 | tf_op jit(solution)/shard_map/ppermute | solution.py:377
  70.4 19.3 %collective-permute-done.10 = bf16[2048,256]{1,0:T(8,128)(2,1)S(1)} collective-permute-done((bf16[2048,256]{1,0:T(8,128)(2,1)S(1)}, bf16[2048,256]{1,0:T(8,128)(2,1)S(1)}, u32[]{:S(2)}, u32[]{:S(2)}) %collective-permute-start.10) | collective-permute-done | bytes 1048608 | tf_op jit(solution)/shard_map/ppermute | solution.py:377
  91.9 19.7 %collective-permute-start.15 = (bf16[1024,256]{1,0:T(8,128)(2,1)S(1)}, bf16[1024,256]{1,0:T(8,128)(2,1)S(1)}, u32[]{:S(2)}, u32[]{:S(2)}) collective-permute-start(bf16[1024,256]{1,0:T(8,128)(2,1)S(1)} %slice.67), channel_id=1, source_target_pairs={{8,0},{16,8},{24,16},{28,24},{20,28},{12,20},{4,12},{0,4},{9,1},{1... | collective-permute-start | bytes 1572872 | tf_op jit(solution)/shard_map/ppermute | solution.py:377
  122.6 12.6 %collective-permute-done.16 = bf16[384,2048]{1,0:T(8,128)(2,1)S(1)} collective-permute-done((bf16[384,2048]{1,0:T(8,128)(2,1)S(1)}, bf16[384,2048]{1,0:T(8,128)(2,1)S(1)}, u32[]{:S(2)}, u32[]{:S(2)}) %collective-permute-start.16) | collective-permute-done | bytes 1572896 | tf_op jit(solution)/shard_map/ppermute | solution.py:421
  144.9 27.0 %collective-permute-done.19 = bf16[384,2048]{1,0:T(8,128)(2,1)} collective-permute-done((bf16[384,2048]{1,0:T(8,128)(2,1)S(1)}, bf16[384,2048]{1,0:T(8,128)(2,1)}, u32[]{:S(2)}, u32[]{:S(2)}) %collective-permute-start.19) | collective-permute-done | bytes 1572896 | tf_op jit(solution)/shard_map/ppermute | solution.py:462
  173.7 11.3 %maximum_maximum_fusion.refs_0_.refs_1_.refs_2_.refs_3_ = bf16[768,4096]{1,0:T(8,128)(2,1)} fusion(bf16[384,2048]{1,0:T(8,128)(2,1)} %collective-permute-done.19, bf16[384,2048]{1,0:T(8,128)(2,1)S(1)} %collective-permute-done.16, bf16[768,2048]{1,0:T(8,128)(2,1)} %broadcast_select_fusion.1), kind=kLoop, calls=%fused_computation.10 | loop fusion | flops 18874368 | bytes 12582912 | tf_op jit(solution)/shard_map/concatenate | solution.py:468
  185.0 23.3 %mix_matmul.1.mix_ref = f32[768,2048]{1,0:T(8,128)} custom-call(s32[2,8]{1,0:T(2,128)S(1)} %pad_add_fusion.2.at_ref, bf16[768,4096]{1,0:T(8,128)(2,1)} %maximum_maximum_fusion.refs_0_.refs_1_.refs_2_.refs_3_, bf16[768,4096]{1,0:T(8,128)(2,1)} %maximum_maximum_fusion.refs_0_.refs_1_.refs_2_.refs_3_, ...), custom_call_target="tpu_custom_call" | custom-call | flops 1024 | bytes 1024 | tf_op jit(solution)/shard_map/mix_matmul/pallas_call | solution.py:214
  230.6 21.4 %backward_conv.1 = (f32[768,2048]{1,0:T(8,128)}, bf16[768,2048]{1,0:T(8,128)(2,1)}) custom-call(f32[128,256]{1,0:T(8,128)S(1)} %concatenate.32.base_ref, s32[1,896]{1,0:T(1,128)S(1)} %broadcast_in_dim.45.last_ref, bf16[768,2048]{1,0:T(8,128)(2,1)} %broadcast_select_fusion.keys_ref, bf16[768,2048]{1,0:T(8,128)(2,1)} %copy-done.1, f32[768,2048]{1,0:T(8,128)} %mix_matmul.1.mix_ref), custom_call_target="tpu_custom_call" | custom-call | flops 1024 | bytes 1024 | tf_op jit(solution)/shard_map/backward_conv/pallas_call | solution.py:134
  252.0 6.0 %backward_ending.1 = (f32[768,2048]{1,0:T(8,128)}, bf16[768,2048]{1,0:T(8,128)(2,1)}) custom-call(f32[128,256]{1,0:T(8,128)S(1)} %concatenate.32.base_ref, s32[1,896]{1,0:T(1,128)S(1)} %broadcast_in_dim.45.last_ref, bf16[128,2048]{1,0:T(8,128)(2,1)S(1)} %collective-permute-done.28.head_ref, ...), custom_call_target="tpu_custom_call", output_to_operand_aliasing={{0}: (6, {}), {1}: (7, {})} | custom-call | flops 1024 | bytes 1024 | tf_op jit(solution)/shard_map/backward_ending/pallas_call | solution.py:164
  259.1 39.3 %collective-permute-start.31 = (bf16[768,2048]{1,0:T(8,128)(2,1)}, bf16[768,2048]{1,0:T(8,128)(2,1)}, u32[]{:S(2)}, u32[]{:S(2)}) collective-permute-start(bf16[768,2048]{1,0:T(8,128)(2,1)} %get-tuple-element.139.refs_4_), channel_id=1, source_target_pairs={{0,1},{1,0},{2,3},{3,2},{4,5},{5,4},{6,7},{7,6},{8,9},{9,8},{10,11... | collective-permute-start | bytes 9437192 | tf_op jit(solution)/shard_map/ppermute | solution.py:374
  301.3 15.4 %forward_conv.2 = (bf16[768,1024]{1,0:T(8,128)(2,1)}, bf16[768,1024]{1,0:T(8,128)(2,1)}) custom-call(f32[128,256]{1,0:T(8,128)S(1)} %maximum_maximum_fusion.1.base_ref, s32[768,1]{1,0:T(8,128)S(1)} %copy.18.last_ref, bf16[128,2048]{1,0:T(8,128)(2,1)S(1)} %collective-permute-done.13.tail_ref, bf16[768,2048]{1,0:T(8,128)(2,1)} %broadcast_select_fusion.keys_ref, ...), custom_call_target="tpu_custom_call" | custom-call | flops 1024 | bytes 1024 | tf_op jit(solution)/shard_map/forward_conv/pallas_call | solution.py:134
  317.2 4.8 collective-permute-done.29.refs_5_
  327.3 15.3 %forward_conv.3 = (bf16[768,1024]{1,0:T(8,128)(2,1)}, bf16[768,1024]{1,0:T(8,128)(2,1)}) custom-call(f32[128,256]{1,0:T(8,128)S(1)} %maximum_maximum_fusion.1.base_ref, s32[768,1]{1,0:T(8,128)S(1)} %copy.18.last_ref, bf16[128,2048]{1,0:T(8,128)(2,1)S(1)} %collective-permute-done.13.tail_ref, bf16[768,2048]{1,0:T(8,128)(2,1)} %broadcast_select_fusion.keys_ref, ...), custom_call_target="tpu_custom_call" | custom-call | flops 1024 | bytes 1024 | tf_op jit(solution)/shard_map/forward_conv/pallas_call | solution.py:134
  348.9 23.5 %project.4 = (bf16[3,768,256]{2,1,0:T(8,128)(2,1)S(1)}, bf16[3,768,256]{2,1,0:T(8,128)(2,1)}) custom-call(bf16[768,1024]{1,0:T(8,128)(2,1)} %get-tuple-element.134.refs_0_, bf16[768,1024]{1,0:T(8,128)(2,1)} %get-tuple-element.136.refs_1_, bf16[768,1024]{1,0:T(8,128)(2,1)} %get-tuple-element.137.refs_2_, bf16[768,1024]{1,0:T(8,128)(2,1)} %get-tuple-element.138.refs_3_, ...), custom_call_target="tpu_custom_call" | custom-call | flops 1024 | bytes 1024 | tf_op jit(solution)/shard_map/project/pallas_call | solution.py:270
  373.9 17.5 %project.5 = (bf16[2,768,256]{2,1,0:T(8,128)(2,1)S(1)}, bf16[2,768,256]{2,1,0:T(8,128)(2,1)S(1)}) custom-call(bf16[768,1024]{1,0:T(8,128)(2,1)} %get-tuple-element.134.refs_0_, bf16[768,1024]{1,0:T(8,128)(2,1)} %get-tuple-element.136.refs_1_, bf16[768,1024]{1,0:T(8,128)(2,1)} %get-tuple-element.137.refs_2_, bf16[768,1024]{1,0:T(8,128)(2,1)} %get-tuple-element.138.refs_3_, ...), custom_call_target="tpu_custom_call" | custom-call | flops 1024 | bytes 1024 | tf_op jit(solution)/shard_map/project/pallas_call | solution.py:270
  392.3 9.5 %collective-permute-done.36 = bf16[3,768,256]{2,1,0:T(8,128)(2,1)S(1)} collective-permute-done((bf16[3,768,256]{2,1,0:T(8,128)(2,1)S(1)}, bf16[3,768,256]{2,1,0:T(8,128)(2,1)S(1)}, u32[]{:S(2)}, u32[]{:S(2)}) %collective-permute-start.36) | collective-permute-done | bytes 1179680 | tf_op jit(solution)/shard_map/ppermute | solution.py:519
  407.9 17.2 %project.6 = (bf16[2,768,256]{2,1,0:T(8,128)(2,1)S(1)}, bf16[2,768,256]{2,1,0:T(8,128)(2,1)S(1)}) custom-call(bf16[768,1024]{1,0:T(8,128)(2,1)} %get-tuple-element.134.refs_0_, bf16[768,1024]{1,0:T(8,128)(2,1)} %get-tuple-element.136.refs_1_, bf16[768,1024]{1,0:T(8,128)(2,1)} %get-tuple-element.137.refs_2_, bf16[768,1024]{1,0:T(8,128)(2,1)} %get-tuple-element.138.refs_3_, ...), custom_call_target="tpu_custom_call" | custom-call | flops 1024 | bytes 1024 | tf_op jit(solution)/shard_map/project/pallas_call | solution.py:270
  426.1 13.4 %collective-permute-done.38 = bf16[3,128,2048]{2,1,0:T(8,128)(2,1)S(1)} collective-permute-done((bf16[3,128,2048]{2,1,0:T(8,128)(2,1)S(1)}, bf16[3,128,2048]{2,1,0:T(8,128)(2,1)S(1)}, u32[]{:S(2)}, u32[]{:S(2)}) %collective-permute-start.38) | collective-permute-done | bytes 1572896 | tf_op jit(solution)/shard_map/ppermute | solution.py:377
  446.3 12.1 %project.7 = (bf16[1,768,256]{2,1,0:T(8,128)(2,1)S(1)}, bf16[1,768,256]{2,1,0:T(8,128)(2,1)S(1)}) custom-call(bf16[768,1024]{1,0:T(8,128)(2,1)} %get-tuple-element.134.refs_0_, bf16[768,1024]{1,0:T(8,128)(2,1)} %get-tuple-element.136.refs_1_, bf16[768,1024]{1,0:T(8,128)(2,1)} %get-tuple-element.137.refs_2_, bf16[768,1024]{1,0:T(8,128)(2,1)} %get-tuple-element.138.refs_3_, ...), custom_call_target="tpu_custom_call" | custom-call | flops 1024 | bytes 1024 | tf_op jit(solution)/shard_map/project/pallas_call | solution.py:270
  463.7 7.4 %collective-permute-done.41 = bf16[1,768,256]{2,1,0:T(8,128)(2,1)} collective-permute-done((bf16[1,768,256]{2,1,0:T(8,128)(2,1)}, bf16[1,768,256]{2,1,0:T(8,128)(2,1)}, u32[]{:S(2)}, u32[]{:S(2)}) %collective-permute-start.41) | collective-permute-done | bytes 393248 | tf_op jit(solution)/shard_map/ppermute | solution.py:519
  478.2 9.0 %pick.1 = (bf16[768,2048]{1,0:T(8,128)(2,1)}, f32[768,1]{1,0:T(8,128)S(1)}) custom-call(s32[3,8]{1,0:T(4,128)S(1)} %pad_add_fusion.1.at_ref, bf16[8,768,256]{2,1,0:T(8,128)(2,1)} %pad_maximum_fusion.1.own_ref, bf16[8,768,256]{2,1,0:T(8,128)(2,1)} %pad_maximum_fusion.2.sib_ref, bf16[768,2048]{1,0:T(8,128)(2,1)} %input_ref.1, ...), custom_call_target="tpu_custom_call" | custom-call | flops 1024 | bytes 1024 | tf_op jit(solution)/shard_map/pick/pallas_call | solution.py:313
  490.1 5.4 %fusion.4 = bf16[768,2048]{1,0:T(8,128)(2,1)} fusion(bf16[768,2048]{1,0:T(8,128)(2,1)S(1)} %copy-done.2, bf16[768,2048]{1,0:T(8,128)(2,1)} %get-tuple-element.161, bf16[768,2048]{1,0:T(8,128)(2,1)} %param.13, f32[768]{0:T(1024)S(1)} %get-tuple-element.165, f32[768]{0:T(1024)S(1)} %get-tuple-element.164, f32[2048]{0:T(1024)S(1)} %convert_element_type.85, ...), kind=kLoop, calls=%fused_computation.9 | loop fusion | flops 17301504 | bytes 12600320 | tf_op jit(solution)/shard_map/convert_element_type | solution.py:570
  (201 shorter events, 125.7 us)
Async XLA Ops:
  21.4 68.7 %collective-permute-start.11 = (bf16[3,256,2048]{2,1,0:T(8,128)(2,1)}, bf16[3,256,2048]{2,1,0:T(8,128)(2,1)}, u32[]{:S(2)}, u32[]{:S(2)}) collective-permute-start(bf16[3,256,2048]{2,1,0:T(8,128)(2,1)} %bitcast.59), channel_id=1, source_target_pairs={{1,2},{2,1},{5,6},{6,5},{9,10},{10,9},{13,14},{14,13},{17,18},{18,... | collective-permute-start | bytes 9437192 | tf_op jit(solution)/shard_map/ppermute | solution.py:368
  23.8 66.3 %collective-permute-start.12 = (bf16[768,2048]{1,0:T(8,128)(2,1)}, bf16[768,2048]{1,0:T(8,128)(2,1)}, u32[]{:S(2)}, u32[]{:S(2)}) collective-permute-start(bf16[768,2048]{1,0:T(8,128)(2,1)} %param.13), channel_id=1, source_target_pairs={{1,2},{2,1},{5,6},{6,5},{9,10},{10,9},{13,14},{14,13},{17,18},{18,... | collective-permute-start | bytes 9437192 | tf_op jit(solution)/shard_map/ppermute | solution.py:368
  26.1 44.4 %collective-permute-start.13 = (bf16[128,2048]{1,0:T(8,128)(2,1)S(1)}, bf16[128,2048]{1,0:T(8,128)(2,1)S(1)}, u32[]{:S(2)}, u32[]{:S(2)}) collective-permute-start(bf16[128,2048]{1,0:T(8,128)(2,1)S(1)} %multiply_convert_fusion.1), channel_id=1, source_target_pairs={{0,1},{1,3},{2,4},{3,6},{4,5},{5,7},{6,8},{7,10},{8,9},{9,11},{10,... | collective-permute-start | bytes 1572872 | tf_op jit(solution)/shard_map/ppermute | solution.py:393
  90.2 31.4 %collective-permute-start.14 = (bf16[1024,256]{1,0:T(8,128)(2,1)S(1)}, bf16[1024,256]{1,0:T(8,128)(2,1)S(1)}, u32[]{:S(2)}, u32[]{:S(2)}) collective-permute-start(bf16[1024,256]{1,0:T(8,128)(2,1)S(1)} %slice.66), channel_id=1, source_target_pairs={{0,8},{8,16},{16,24},{24,28},{28,20},{20,12},{12,4},{4,0},{1,9},{9... | collective-permute-start | bytes 1572872 | tf_op jit(solution)/shard_map/ppermute | solution.py:377
  91.9 29.6 %collective-permute-start.15 = (bf16[1024,256]{1,0:T(8,128)(2,1)S(1)}, bf16[1024,256]{1,0:T(8,128)(2,1)S(1)}, u32[]{:S(2)}, u32[]{:S(2)}) collective-permute-start(bf16[1024,256]{1,0:T(8,128)(2,1)S(1)} %slice.67), channel_id=1, source_target_pairs={{8,0},{16,8},{24,16},{28,24},{20,28},{12,20},{4,12},{0,4},{9,1},{1... | collective-permute-start | bytes 1572872 | tf_op jit(solution)/shard_map/ppermute | solution.py:377
  135.2 49.8 %collective-permute-start.20 = (bf16[8,2048,256]{2,1,0:T(8,128)(2,1)}, bf16[8,2048,256]{2,1,0:T(8,128)(2,1)}, u32[]{:S(2)}, u32[]{:S(2)}) collective-permute-start(bf16[8,2048,256]{2,1,0:T(8,128)(2,1)} %fusion.5.refs_4_), channel_id=1, source_target_pairs={{0,1},{1,0},{2,3},{3,2},{4,5},{5,4},{6,7},{7,6},{8,9},{9,8},{10,11... | collective-permute-start | bytes 25165832 | tf_op jit(solution)/shard_map/ppermute | solution.py:374
  136.7 35.2 %collective-permute-start.19 = (bf16[384,2048]{1,0:T(8,128)(2,1)S(1)}, bf16[384,2048]{1,0:T(8,128)(2,1)}, u32[]{:S(2)}, u32[]{:S(2)}) collective-permute-start(bf16[384,2048]{1,0:T(8,128)(2,1)S(1)} %slice.73), channel_id=1, source_target_pairs={{0,2},{1,0},{2,3},{3,1},{4,6},{5,4},{6,7},{7,5},{8,10},{9,8},{10,1... | collective-permute-start | bytes 4718600 | tf_op jit(solution)/shard_map/ppermute | solution.py:462
  139.2 69.1 %collective-permute-start.21 = (bf16[768,2048]{1,0:T(8,128)(2,1)}, bf16[768,2048]{1,0:T(8,128)(2,1)}, u32[]{:S(2)}, u32[]{:S(2)}) collective-permute-start(bf16[768,2048]{1,0:T(8,128)(2,1)} %param.17), channel_id=1, source_target_pairs={{1,2},{2,1},{5,6},{6,5},{9,10},{10,9},{13,14},{14,13},{17,18},{18,... | collective-permute-start | bytes 9437192 | tf_op jit(solution)/shard_map/ppermute | solution.py:368
  141.5 70.8 %collective-permute-start.17 = (bf16[3,256,2048]{2,1,0:T(8,128)(2,1)}, bf16[3,256,2048]{2,1,0:T(8,128)(2,1)}, u32[]{:S(2)}, u32[]{:S(2)}) collective-permute-start(bf16[3,256,2048]{2,1,0:T(8,128)(2,1)} %broadcast_select_fusion.2.refs_10_), channel_id=1, source_target_pairs={{0,8},{8,16},{16,24},{24,28},{28,20},{20,12},{12,4},{4,0},{1,9},{9... | collective-permute-start | bytes 9437192 | tf_op jit(solution)/shard_map/ppermute | solution.py:377
  143.2 70.3 %collective-permute-start.18 = (bf16[3,256,2048]{2,1,0:T(8,128)(2,1)}, bf16[3,256,2048]{2,1,0:T(8,128)(2,1)}, u32[]{:S(2)}, u32[]{:S(2)}) collective-permute-start(bf16[3,256,2048]{2,1,0:T(8,128)(2,1)} %broadcast_select_fusion.2.refs_10_), channel_id=1, source_target_pairs={{8,0},{16,8},{24,16},{28,24},{20,28},{12,20},{4,12},{0,4},{9,1},{1... | collective-permute-start | bytes 9437192 | tf_op jit(solution)/shard_map/ppermute | solution.py:377
  171.9 36.4 %collective-permute-start.22 = (bf16[384,2048]{1,0:T(8,128)(2,1)}, bf16[384,2048]{1,0:T(8,128)(2,1)}, u32[]{:S(2)}, u32[]{:S(2)}) collective-permute-start(bf16[384,2048]{1,0:T(8,128)(2,1)} %slice.74), channel_id=1, source_target_pairs={{1,2},{2,1},{5,6},{6,5},{9,10},{10,9},{13,14},{14,13},{17,18},{18,... | collective-permute-start | bytes 4718600 | tf_op jit(solution)/shard_map/ppermute | solution.py:368
  214.6 102.7 %collective-permute-start.23 = (bf16[3,256,2048]{2,1,0:T(8,128)(2,1)}, bf16[3,256,2048]{2,1,0:T(8,128)(2,1)}, u32[]{:S(2)}, u32[]{:S(2)}) collective-permute-start(bf16[3,256,2048]{2,1,0:T(8,128)(2,1)} %collective-permute-done.17.refs_11_), channel_id=1, source_target_pairs={{0,8},{8,16},{16,24},{24,28},{28,20},{20,12},{12,4},{4,0},{1,9},{9... | collective-permute-start | bytes 9437192 | tf_op jit(solution)/shard_map/ppermute | solution.py:377
  216.2 101.0 %collective-permute-start.24 = (bf16[3,256,2048]{2,1,0:T(8,128)(2,1)}, bf16[3,256,2048]{2,1,0:T(8,128)(2,1)}, u32[]{:S(2)}, u32[]{:S(2)}) collective-permute-start(bf16[3,256,2048]{2,1,0:T(8,128)(2,1)} %collective-permute-done.18.refs_12_), channel_id=1, source_target_pairs={{8,0},{16,8},{24,16},{28,24},{20,28},{12,20},{4,12},{0,4},{9,1},{1... | collective-permute-start | bytes 9437192 | tf_op jit(solution)/shard_map/ppermute | solution.py:377
  218.6 39.3 %collective-permute-start.26 = (bf16[768,1024]{1,0:T(8,128)(2,1)}, bf16[768,1024]{1,0:T(8,128)(2,1)S(1)}, u32[]{:S(2)}, u32[]{:S(2)}) collective-permute-start(bf16[768,1024]{1,0:T(8,128)(2,1)} %get-tuple-element.168), channel_id=1, source_target_pairs={{1,2},{2,1},{5,6},{6,5},{9,10},{10,9},{13,14},{14,13},{17,18},{18,... | collective-permute-start | bytes 4718600 | tf_op jit(solution)/shard_map/ppermute | solution.py:368
  219.4 38.6 %collective-permute-start.27 = (bf16[768,1024]{1,0:T(8,128)(2,1)}, bf16[768,1024]{1,0:T(8,128)(2,1)S(1)}, u32[]{:S(2)}, u32[]{:S(2)}) collective-permute-start(bf16[768,1024]{1,0:T(8,128)(2,1)} %get-tuple-element.167), channel_id=1, source_target_pairs={{1,2},{2,1},{5,6},{6,5},{9,10},{10,9},{13,14},{14,13},{17,18},{18,... | collective-permute-start | bytes 4718600 | tf_op jit(solution)/shard_map/ppermute | solution.py:368
  259.1 63.7 %collective-permute-start.31 = (bf16[768,2048]{1,0:T(8,128)(2,1)}, bf16[768,2048]{1,0:T(8,128)(2,1)}, u32[]{:S(2)}, u32[]{:S(2)}) collective-permute-start(bf16[768,2048]{1,0:T(8,128)(2,1)} %get-tuple-element.139.refs_4_), channel_id=1, source_target_pairs={{0,1},{1,0},{2,3},{3,2},{4,5},{5,4},{6,7},{7,6},{8,9},{9,8},{10,11... | collective-permute-start | bytes 9437192 | tf_op jit(solution)/shard_map/ppermute | solution.py:374
  322.8 79.1 %collective-permute-start.32 = (bf16[3,256,2048]{2,1,0:T(8,128)(2,1)}, bf16[3,256,2048]{2,1,0:T(8,128)(2,1)}, u32[]{:S(2)}, u32[]{:S(2)}) collective-permute-start(bf16[3,256,2048]{2,1,0:T(8,128)(2,1)} %collective-permute-done.23.refs_10_), channel_id=1, source_target_pairs={{0,8},{8,16},{16,24},{24,28},{28,20},{20,12},{12,4},{4,0},{1,9},{9... | collective-permute-start | bytes 9437192 | tf_op jit(solution)/shard_map/ppermute | solution.py:377
  324.6 77.3 %collective-permute-start.33 = (bf16[3,256,2048]{2,1,0:T(8,128)(2,1)}, bf16[3,256,2048]{2,1,0:T(8,128)(2,1)}, u32[]{:S(2)}, u32[]{:S(2)}) collective-permute-start(bf16[3,256,2048]{2,1,0:T(8,128)(2,1)} %collective-permute-done.24.refs_11_), channel_id=1, source_target_pairs={{8,0},{16,8},{24,16},{28,24},{20,28},{12,20},{4,12},{0,4},{9,1},{1... | collective-permute-start | bytes 9437192 | tf_op jit(solution)/shard_map/ppermute | solution.py:377
  373.8 28.1 %collective-permute-start.36 = (bf16[3,768,256]{2,1,0:T(8,128)(2,1)S(1)}, bf16[3,768,256]{2,1,0:T(8,128)(2,1)S(1)}, u32[]{:S(2)}, u32[]{:S(2)}) collective-permute-start(bf16[3,768,256]{2,1,0:T(8,128)(2,1)S(1)} %get-tuple-element.169), channel_id=1, source_target_pairs={{0,2},{2,0},{1,3},{3,1},{4,6},{6,4},{5,7},{7,5},{8,10},{10,8},{9,1... | collective-permute-start | bytes 3538952 | tf_op jit(solution)/shard_map/ppermute | solution.py:519
  403.5 36.0 %collective-permute-start.38 = (bf16[3,128,2048]{2,1,0:T(8,128)(2,1)S(1)}, bf16[3,128,2048]{2,1,0:T(8,128)(2,1)S(1)}, u32[]{:S(2)}, u32[]{:S(2)}) collective-permute-start(bf16[3,128,2048]{2,1,0:T(8,128)(2,1)S(1)} %slice.82), channel_id=1, source_target_pairs={{0,8},{8,16},{16,24},{24,28},{28,20},{20,12},{12,4},{4,0},{1,9},{9... | collective-permute-start | bytes 4718600 | tf_op jit(solution)/shard_map/ppermute | solution.py:377
  406.0 35.4 %collective-permute-start.39 = (bf16[3,128,2048]{2,1,0:T(8,128)(2,1)S(1)}, bf16[3,128,2048]{2,1,0:T(8,128)(2,1)S(1)}, u32[]{:S(2)}, u32[]{:S(2)}) collective-permute-start(bf16[3,128,2048]{2,1,0:T(8,128)(2,1)S(1)} %slice.83), channel_id=1, source_target_pairs={{8,0},{16,8},{24,16},{28,24},{20,28},{12,20},{4,12},{0,4},{9,1},{1... | collective-permute-start | bytes 4718600 | tf_op jit(solution)/shard_map/ppermute | solution.py:377
  407.3 35.3 %collective-permute-start.37 = (bf16[2,768,256]{2,1,0:T(8,128)(2,1)}, bf16[2,768,256]{2,1,0:T(8,128)(2,1)}, u32[]{:S(2)}, u32[]{:S(2)}) collective-permute-start(bf16[2,768,256]{2,1,0:T(8,128)(2,1)} %get-tuple-element.150), channel_id=1, source_target_pairs={{0,2},{2,0},{1,3},{3,1},{4,6},{6,4},{5,7},{7,5},{8,10},{10,8},{9,1... | collective-permute-start | bytes 2359304 | tf_op jit(solution)/shard_map/ppermute | solution.py:519
  407.8 67.1 %collective-permute-start.42 = (bf16[3,768,256]{2,1,0:T(8,128)(2,1)S(1)}, bf16[3,768,256]{2,1,0:T(8,128)(2,1)}, u32[]{:S(2)}, u32[]{:S(2)}) collective-permute-start(bf16[3,768,256]{2,1,0:T(8,128)(2,1)S(1)} %add_convert_fusion), channel_id=1, source_target_pairs={{0,1},{1,0},{2,3},{3,2},{4,5},{5,4},{6,7},{7,6},{8,9},{9,8},{10,11... | collective-permute-start | bytes 3538952 | tf_op jit(solution)/shard_map/ppermute | solution.py:556
  446.3 28.6 %collective-permute-start.43 = (bf16[2,768,256]{2,1,0:T(8,128)(2,1)S(1)}, bf16[2,768,256]{2,1,0:T(8,128)(2,1)}, u32[]{:S(2)}, u32[]{:S(2)}) collective-permute-start(bf16[2,768,256]{2,1,0:T(8,128)(2,1)S(1)} %add_convert_fusion.2), channel_id=1, source_target_pairs={{0,1},{1,0},{2,3},{3,2},{4,5},{5,4},{6,7},{7,6},{8,9},{9,8},{10,11... | collective-permute-start | bytes 2359304 | tf_op jit(solution)/shard_map/ppermute | solution.py:556
  (45 other events, 588.8 us)
